TPU v7x, 32 devices: a whole 2x2x4 slice. The times are simulated.
32 devices in a mesh: dom: 8 (over z, x), sub: 4 (over y, core).
Axes of the slice: x: 2, y: 2, z: 4, core: 2. Of those that a mesh axis runs over, the one named last changes fastest.
Arguments:
- state: float32 [5, 64, 1024], P(None, None, ('dom', 'sub')), may hold values from -0.9 to 0.9
- adjoint_final: float32 [5, 64, 1024], P(None, None, ('dom', 'sub')), may hold values from -6 to 6
- send_slot: int32 [32, 192], P(('dom', 'sub')), may hold values from 0 to 192, as said below
- ext_index: int32 [6, 1024], P(None, ('dom', 'sub')), may hold values from 0 to 384, as said below
- ext_perm: int32 [6, 1024], P(None, ('dom', 'sub')), may hold values from 0 to 7
Outputs:
- state_end: float32 [5, 64, 1024], P(None, None, ('dom', 'sub'))
- adjoint_start: float32 [5, 64, 1024], P(None, None, ('dom', 'sub'))
Inputs may be any that keep to these rules, and one draw needn't show every extreme that they name: `send_slot`: A value of 192 marks an empty slot, which carries zeros; the share of occupied slots differs from device to device, and device 0 fills all its slots. `ext_index`: values below 192 name a face of the same device, values from 192 to 383 a received slot, and 384 a wall.
All inputs are finite; a program needn't handle non-finite values.
Results may differ from a plain program's by a relative error of at most 0.0006.
Values may be sent and summed in bfloat16 or wider, within the bound.
A program may use at most 64 MiB of HBM per device.

v0:
```python
import jax
import jax.numpy as jnp
import numpy as np
from jax import lax
from jax.sharding import PartitionSpec as P

step_size = 0.02
mean_flow = 0.3
penalty = 2.0
metric = 2.0
lift_factor = 12.0


def as_sent(x):

    def short(part):
        return part.astype(jnp.bfloat16) if part.dtype == jnp.float32 else part

    return jax.tree.map(short, x)


def from_behind(value, axis, steps):
    count = lax.axis_size(axis)
    pairs = [(source, (source + steps) % count) for source in range(count)]
    return lax.ppermute(value, axis, pairs)


def derivative_table():
    points = np.array([-1.0, -1.0 / np.sqrt(5.0), 1.0 / np.sqrt(5.0), 1.0])
    products = np.array(
        [
            np.prod([points[target] - points[source] for source in range(4) if source != target])
            for target in range(4)
        ]
    )
    result = np.zeros((4, 4))
    for target in range(4):
        for source in range(4):
            if target != source:
                result[target, source] = products[target] / (
                    products[source] * (points[target] - points[source])
                )
        result[target, target] = -np.sum(result[target])
    return result.astype(np.float32)


def symmetry_table():
    result = np.zeros((8, 16), np.int32)
    for symmetry in range(8):
        layout = np.arange(16).reshape(4, 4)
        if symmetry & 4:
            layout = layout.T
        if symmetry & 1:
            layout = layout[::-1]
        if symmetry & 2:
            layout = layout[:, ::-1]
        result[symmetry] = layout.reshape(-1)
    return result


def normal_table():
    result = np.zeros((3, 6), np.float32)
    for facet in range(6):
        result[facet // 2, facet] = 2.0 * (facet % 2) - 1.0
    return result


def flux_along(fields, drift, normal_speed, pressure_weights):
    density = fields[0]
    pressure = fields[4]
    components = [drift * density + (1.0 + density) * normal_speed]
    for member in range(3):
        velocity = fields[1 + member]
        components.append(
            drift * velocity + velocity * normal_speed + pressure_weights[member] * pressure
        )
    components.append(drift * pressure + (1.0 + pressure) * normal_speed)
    return jnp.stack(components)


def volume_term(field):
    elements = field.shape[2]
    derivative = derivative_table()
    table = jnp.asarray(derivative, jnp.float32)
    merged = 4 * elements
    total = jnp.zeros((5, 4, 4, merged), jnp.float32)
    for direction in range(3):
        drift = mean_flow if direction == 0 else 0.0
        weights = [1.0 if member == direction else 0.0 for member in range(3)]
        flux = flux_along(field, drift, field[1 + direction], weights).reshape(5, 4, 4, merged)
        if direction == 0:
            total = total + jnp.einsum(
                "ai,vijm->vajm", table, flux, precision=lax.Precision.HIGHEST
            )
        elif direction == 1:
            total = total + jnp.einsum(
                "aj,vijm->viam", table, flux, precision=lax.Precision.HIGHEST
            )
        else:
            blocks = [flux[..., index * elements : (index + 1) * elements] for index in range(4)]
            outputs = []
            for target in range(4):
                accum = float(derivative[target, 0]) * blocks[0]
                for index in range(1, 4):
                    accum = accum + float(derivative[target, index]) * blocks[index]
                outputs.append(accum)
            total = total + jnp.concatenate(outputs, axis=3)
    return -metric * total.reshape(5, 64, elements)


def normal_flux(trace):
    normals = normal_table()
    weights = [jnp.asarray(normals[member], jnp.float32)[:, None] for member in range(3)]
    normal_speed = weights[0] * trace[1] + weights[1] * trace[2] + weights[2] * trace[3]
    return flux_along(trace, mean_flow * weights[0], normal_speed, weights)


def face_traces(field):
    elements = field.shape[2]
    cube = field.reshape(5, 4, 4, 4, elements)
    surfaces = [
        cube[:, 0],
        cube[:, 3],
        cube[:, :, 0],
        cube[:, :, 3],
        cube[:, :, :, 0],
        cube[:, :, :, 3],
    ]
    return jnp.stack([surface.reshape(5, 16, elements) for surface in surfaces], axis=2).reshape(
        5, 16, 6 * elements
    )


def pack_sends(field, slots, n_sub):
    traces = face_traces(field)
    padded = jnp.concatenate([traces, jnp.zeros((5, 16, 1), traces.dtype)], axis=2)
    picked = jnp.take(padded, slots, axis=2)
    return picked.transpose(2, 0, 1).reshape(3, n_sub, -1)


def residual(field, arrived, ext_index, ext_perm):
    elements = field.shape[2]
    symmetries = symmetry_table()
    traces = face_traces(field)
    incoming = arrived.reshape(-1, 5, 16).transpose(1, 2, 0)
    lookup = jnp.concatenate([traces, incoming, jnp.zeros((5, 16, 1), traces.dtype)], axis=2)
    count = lookup.shape[2]
    flattened = ext_index.reshape(-1)
    orient = ext_perm.reshape(-1)
    matches = orient[None, None, :] == jnp.arange(8, dtype=jnp.int32)[:, None, None]
    node_map = jnp.sum(jnp.where(matches, jnp.asarray(symmetries)[:, :, None], 0), axis=0).astype(
        jnp.int32
    )
    gather_index = node_map * count + flattened[None, :]
    exterior = jnp.take(lookup.reshape(5, -1), gather_index, axis=1)
    direction = jnp.arange(6 * elements, dtype=jnp.int32) // elements // 2
    component = jnp.arange(5, dtype=jnp.int32)[:, None]
    mirror_sign = jnp.where(component == 1 + direction[None, :], -1.0, 1.0).astype(jnp.float32)[
        :, None, :
    ]
    at_wall = (flattened == count - 1)[None, None, :]
    exterior = jnp.where(at_wall, traces * mirror_sign, exterior)
    interior = traces.reshape(5, 16, 6, elements)
    exterior = exterior.reshape(5, 16, 6, elements)
    penalty_jump = 0.5 * (normal_flux(interior) - normal_flux(exterior)) + 0.5 * penalty * (
        exterior - interior
    )
    jumps = penalty_jump.reshape(5, 4, 4, 6, elements)
    lifted = jnp.zeros((5, 4, 4, 4, elements), jnp.float32)
    lifted = lifted.at[:, 0].add(jumps[:, :, :, 0])
    lifted = lifted.at[:, 3].add(jumps[:, :, :, 1])
    lifted = lifted.at[:, :, 0].add(jumps[:, :, :, 2])
    lifted = lifted.at[:, :, 3].add(jumps[:, :, :, 3])
    lifted = lifted.at[:, :, :, 0].add(jumps[:, :, :, 4])
    lifted = lifted.at[:, :, :, 3].add(jumps[:, :, :, 5])
    return volume_term(field) + lift_factor * lifted.reshape(5, 64, elements)


def sub_forward(buffer):
    return lax.all_to_all(buffer, "sub", split_axis=1, concat_axis=1, tiled=True)


def sub_backward(buffer):
    return lax.all_to_all(as_sent(buffer), "sub", split_axis=1, concat_axis=1, tiled=True).astype(
        buffer.dtype
    )


def dom_forward(buffer):
    pieces = [buffer[0:1], buffer[1:2], buffer[2:3]]
    for group_id, offset in ((0, -1), (2, 1)):
        pieces[group_id] = from_behind(buffer[group_id : group_id + 1], "dom", offset)
    return jnp.concatenate(pieces, axis=0)


def dom_backward(buffer):
    pieces = [buffer[0:1], buffer[1:2], buffer[2:3]]
    for group_id, offset in ((0, 1), (2, -1)):
        pieces[group_id] = from_behind(
            buffer[group_id : group_id + 1].astype(jnp.bfloat16), "dom", offset
        ).astype(jnp.float32)
    return jnp.concatenate(pieces, axis=0)


def forward_move(buffer):
    return dom_forward(sub_forward(buffer))


def backward_move(buffer):
    return sub_backward(dom_backward(buffer))


def shards(state, adjoint_final, send_slot, ext_index, ext_perm):
    n_sub = lax.axis_size("sub")
    slots = send_slot.reshape(-1)

    def evaluate(current):
        outgoing = pack_sends(current, slots, n_sub).astype(jnp.bfloat16)
        arrived = forward_move(outgoing).astype(jnp.float32)
        return (residual(current, arrived, ext_index, ext_perm), arrived)

    def pull_back(current, arrived, cotangent):
        _, pullback = jax.vjp(
            lambda first, second: residual(first, second, ext_index, ext_perm), current, arrived
        )
        grad_state, grad_arrived = pullback(cotangent)
        returned = backward_move(grad_arrived)
        _, pack_pullback = jax.vjp(lambda first: pack_sends(first, slots, n_sub), current)
        return grad_state + pack_pullback(returned)[0]

    rate_first, arrived_first = evaluate(state)
    middle = state + step_size * rate_first
    rate_second, arrived_second = evaluate(middle)
    final = 0.5 * state + 0.5 * (middle + step_size * rate_second)
    back_middle = 0.5 * adjoint_final + 0.5 * step_size * pull_back(
        middle, arrived_second, adjoint_final
    )
    back_start = (
        0.5 * adjoint_final + back_middle + step_size * pull_back(state, arrived_first, back_middle)
    )
    return (final, back_start)


def solution(mesh):
    return jax.shard_map(
        shards,
        mesh=mesh,
        in_specs=(
            P(None, None, ("dom", "sub")),
            P(None, None, ("dom", "sub")),
            P(("dom", "sub"), None),
            P(None, ("dom", "sub")),
            P(None, ("dom", "sub")),
        ),
        out_specs=(P(None, None, ("dom", "sub")), P(None, None, ("dom", "sub"))),
        check_vma=False,
    )
```

profile of v0, /device:TPU:0, one launch (start us, length us, event | category | flops | bytes accessed | tf_op | source)
XLA Modules:
  0.0 225.2 jit_solution(11058009783494582195)
XLA Ops:
  6.1 4.2 %all-to-all-start = ((bf16[3,4,1280]{2,0,1:T(4,128)(2,1)}), bf16[3,4,1280]{2,0,1:T(4,128)(2,1)S(1)}, u32[]{:S(2)}, u32[]{:S(2)}) async-start(bf16[3,4,1280]{2,0,1:T(4,128)(2,1)} %copy.1383), calls=%async_computation | async-start | bytes 81920 | tf_op jit(solution)/shard_map/all_to_all | solution.py:180
  18.4 5.1 %collective-permute-start = (bf16[1,4,1280]{2,1,0:T(4,128)(2,1)S(1)}, bf16[1,4,1280]{2,1,0:T(4,128)(2,1)S(1)}, u32[]{:S(2)}, u32[]{:S(2)}) collective-permute-start(bf16[1,4,1280]{2,1,0:T(4,128)(2,1)S(1)} %copy.1576), channel_id=1, source_target_pairs={{0,28},{4,0},{8,4},{12,8},{16,12},{20,16},{24,20},{28,24},{1,29},{... | collective-permute-start | bytes 30728 | tf_op jit(solution)/shard_map/ppermute | solution.py:25
  38.5 2.6 %copy.1388 = f32[5,6160]{0,1:T(8,128)S(1)} copy(f32[5,6160]{1,0:T(8,128)} %reshape.2124) | data formatting | bytes 246400 | tf_op jit(solution)/shard_map/reshape | solution.py:155
  41.1 10.9 %gather_fusion.1 = f32[3072,5]{1,0:T(8,128)} fusion(f32[5,6160]{0,1:T(8,128)S(1)} %copy.1388, s32[3072]{0:T(1024)S(1)} %copy-done.46), kind=kCustom, calls=%fused_computation.1.clone | custom fusion | bytes 135168 | tf_op jit(solution)/shard_map/jit(_take)/gather | solution.py:155
  52.0 2.1 copy.1562
  63.4 3.5 %all-to-all-start.1 = ((bf16[3,4,1280]{2,0,1:T(4,128)(2,1)}), bf16[3,4,1280]{2,0,1:T(4,128)(2,1)S(1)}, u32[]{:S(2)}, u32[]{:S(2)}) async-start(bf16[3,4,1280]{2,0,1:T(4,128)(2,1)} %copy.1414), calls=%async_computation.1 | async-start | bytes 81920 | tf_op jit(solution)/shard_map/all_to_all | solution.py:180
  71.9 4.8 %collective-permute-start.2 = (bf16[1,4,1280]{2,1,0:T(4,128)(2,1)S(1)}, bf16[1,4,1280]{2,1,0:T(4,128)(2,1)S(1)}, u32[]{:S(2)}, u32[]{:S(2)}) collective-permute-start(bf16[1,4,1280]{2,1,0:T(4,128)(2,1)S(1)} %copy.1583), channel_id=1, source_target_pairs={{0,28},{4,0},{8,4},{12,8},{16,12},{20,16},{24,20},{28,24},{1,29},{... | collective-permute-start | bytes 30728 | tf_op jit(solution)/shard_map/ppermute | solution.py:25
  85.1 2.5 %copy.1419 = f32[5,6160]{0,1:T(8,128)S(1)} copy(f32[5,6160]{1,0:T(8,128)} %reshape.2130) | data formatting | bytes 246400 | tf_op jit(solution)/shard_map/reshape | solution.py:155
  87.7 10.9 %gather_fusion.3 = f32[3072,5]{1,0:T(8,128)} fusion(f32[5,6160]{0,1:T(8,128)S(1)} %copy.1419, s32[3072]{0:T(1024)S(1)} %copy-done.46), kind=kCustom, calls=%fused_computation.4.clone | custom fusion | bytes 135168 | tf_op jit(solution)/shard_map/jit(_take)/gather | solution.py:155
  98.6 2.1 copy.1563
  106.8 1.7 copy.1567
  108.5 18.0 %scatter_custom_fusion = f32[5,6160]{0,1:T(8,128)S(1)} fusion(s32[3072]{0:T(1024)} %reshape.2211, f32[3072,5]{1,0:T(8,128)} %bitcast.263, f32[]{:T(128)} %constant.400.clone.1), kind=kCustom, calls=%fused_computation.12 | custom fusion | flops 15360 | bytes 123712 | tf_op jit(solution)/shard_map/transpose(jvp(jit(_take)))/scatter-add | solution.py:155
  126.5 2.2 copy.1472
  132.0 4.8 %collective-permute-start.5 = (bf16[1,4,1280]{2,1,0:T(4,128)(2,1)S(1)}, bf16[1,4,1280]{2,1,0:T(4,128)(2,1)S(1)}, u32[]{:S(2)}, u32[]{:S(2)}) collective-permute-start(bf16[1,4,1280]{2,1,0:T(4,128)(2,1)S(1)} %convert_element_type.93), channel_id=1, source_target_pairs={{0,28},{4,0},{8,4},{12,8},{16,12},{20,16},{24,20},{28,24},{1,29},{... | collective-permute-start | bytes 30728 | tf_op jit(solution)/shard_map/ppermute | solution.py:25
  141.5 3.5 %all-to-all-start.2 = ((bf16[3,4,1280]{2,0,1:T(4,128)(2,1)}), bf16[3,4,1280]{2,0,1:T(4,128)(2,1)S(1)}, u32[]{:S(2)}, u32[]{:S(2)}) async-start(bf16[3,4,1280]{2,0,1:T(4,128)(2,1)} %copy.1481), calls=%async_computation.2 | async-start | bytes 81920 | tf_op jit(solution)/shard_map/all_to_all | solution.py:184
  146.0 2.9 %all-to-all-done.2 = bf16[3,4,1280]{2,0,1:T(4,128)(2,1)S(1)} async-done(((bf16[3,4,1280]{2,0,1:T(4,128)(2,1)}), bf16[3,4,1280]{2,0,1:T(4,128)(2,1)S(1)}, u32[]{:S(2)}, u32[]{:S(2)}) %all-to-all-start.2) | async-done | bytes 30752 | tf_op jit(solution)/shard_map/all_to_all | solution.py:184
  149.2 7.1 %scatter_fusion = f32[5,16,193]{1,0,2:T(8,128)S(1)} fusion(f32[5,16,193]{1,0,2:T(8,128)S(1)} %broadcast_in_dim.132.clone, s32[192]{0:T(256)S(1)} %bitcast.343, f32[192,5,16]{2,1,0:T(8,128)S(1)} %reshape.2159), kind=kCustom, calls=%fused_computation.7 | custom fusion | flops 15360 | bytes 185088 | tf_op jit(solution)/shard_map/transpose(jvp(jit(_take)))/scatter-add | solution.py:137
  171.9 1.7 copy.1571
  173.6 18.0 %scatter_custom_fusion.2 = f32[5,6160]{0,1:T(8,128)S(1)} fusion(s32[3072]{0:T(1024)} %reshape.2211, f32[3072,5]{1,0:T(8,128)} %bitcast.262, f32[]{:T(128)} %constant.400.clone.1), kind=kCustom, calls=%fused_computation.10 | custom fusion | flops 15360 | bytes 123712 | tf_op jit(solution)/shard_map/transpose(jvp(jit(_take)))/scatter-add | solution.py:155
  191.6 2.2 copy.1533
  198.3 4.8 %collective-permute-start.7 = (bf16[1,4,1280]{2,1,0:T(4,128)(2,1)S(1)}, bf16[1,4,1280]{2,1,0:T(4,128)(2,1)S(1)}, u32[]{:S(2)}, u32[]{:S(2)}) collective-permute-start(bf16[1,4,1280]{2,1,0:T(4,128)(2,1)S(1)} %convert_element_type.95), channel_id=1, source_target_pairs={{0,28},{4,0},{8,4},{12,8},{16,12},{20,16},{24,20},{28,24},{1,29},{... | collective-permute-start | bytes 30728 | tf_op jit(solution)/shard_map/ppermute | solution.py:25
  208.6 3.3 %all-to-all-start.3 = ((bf16[3,4,1280]{2,0,1:T(4,128)(2,1)}), bf16[3,4,1280]{2,0,1:T(4,128)(2,1)S(1)}, u32[]{:S(2)}, u32[]{:S(2)}) async-start(bf16[3,4,1280]{2,0,1:T(4,128)(2,1)} %copy.1542), calls=%async_computation.3 | async-start | bytes 81920 | tf_op jit(solution)/shard_map/all_to_all | solution.py:184
  212.8 3.0 %all-to-all-done.3 = bf16[3,4,1280]{2,0,1:T(4,128)(2,1)S(1)} async-done(((bf16[3,4,1280]{2,0,1:T(4,128)(2,1)}), bf16[3,4,1280]{2,0,1:T(4,128)(2,1)S(1)}, u32[]{:S(2)}, u32[]{:S(2)}) %all-to-all-start.3) | async-done | bytes 30752 | tf_op jit(solution)/shard_map/all_to_all | solution.py:184
  216.2 7.1 %scatter_fusion.1 = f32[5,16,193]{1,0,2:T(8,128)S(1)} fusion(f32[5,16,193]{1,0,2:T(8,128)S(1)} %broadcast_in_dim.132, s32[192]{0:T(256)S(1)} %bitcast.344, f32[192,5,16]{2,1,0:T(8,128)S(1)} %reshape.2160), kind=kCustom, calls=%fused_computation.9 | custom fusion | flops 15360 | bytes 185088 | tf_op jit(solution)/shard_map/transpose(jvp(jit(_take)))/scatter-add | solution.py:137
  (682 shorter events, 92.4 us)
Async XLA Ops:
  6.1 12.3 %all-to-all-start = ((bf16[3,4,1280]{2,0,1:T(4,128)(2,1)}), bf16[3,4,1280]{2,0,1:T(4,128)(2,1)S(1)}, u32[]{:S(2)}, u32[]{:S(2)}) async-start(bf16[3,4,1280]{2,0,1:T(4,128)(2,1)} %copy.1383), calls=%async_computation | async-start | bytes 81920 | tf_op jit(solution)/shard_map/all_to_all | solution.py:180
  18.4 18.6 %collective-permute-start = (bf16[1,4,1280]{2,1,0:T(4,128)(2,1)S(1)}, bf16[1,4,1280]{2,1,0:T(4,128)(2,1)S(1)}, u32[]{:S(2)}, u32[]{:S(2)}) collective-permute-start(bf16[1,4,1280]{2,1,0:T(4,128)(2,1)S(1)} %copy.1576), channel_id=1, source_target_pairs={{0,28},{4,0},{8,4},{12,8},{16,12},{20,16},{24,20},{28,24},{1,29},{... | collective-permute-start | bytes 30728 | tf_op jit(solution)/shard_map/ppermute | solution.py:25
  23.5 13.5 %collective-permute-start.1 = (bf16[1,4,1280]{2,1,0:T(4,128)(2,1)S(1)}, bf16[1,4,1280]{2,1,0:T(4,128)(2,1)S(1)}, u32[]{:S(2)}, u32[]{:S(2)}) collective-permute-start(bf16[1,4,1280]{2,1,0:T(4,128)(2,1)S(1)} %copy.1578), channel_id=1, source_target_pairs={{0,4},{4,8},{8,12},{12,16},{16,20},{20,24},{24,28},{28,0},{1,5},{5... | collective-permute-start | bytes 30728 | tf_op jit(solution)/shard_map/ppermute | solution.py:25
  23.5 13.5 %copy-start.26 = (f32[5,4,4,6,32]{4,3,2,1,0:T(8,128)}, f32[5,4,4,6,32]{4,3,2,1,0:T(8,128)S(1)}, u32[]{:S(2)}) copy-start(f32[5,4,4,6,32]{4,3,2,1,0:T(8,128)S(1)} %constant_dynamic-update-slice_fusion.21) | copy-start | bytes 184324
  37.5 16.6 %copy-start.110 = (pred[16,192]{1,0:T(8,128)(4,1)S(1)}, pred[16,192]{1,0:T(8,128)(4,1)}, u32[]{:S(2)}) copy-start(pred[16,192]{1,0:T(8,128)(4,1)} %get-tuple-element.190) | copy-start | bytes 9220
  37.5 16.6 %copy-start.111 = (pred[192]{0:T(512)(128)(4,1)S(1)}, pred[192]{0:T(512)(128)(4,1)}, u32[]{:S(2)}) copy-start(pred[192]{0:T(512)(128)(4,1)} %broadcast_compare_fusion) | copy-start | bytes 580
  38.5 16.8 %copy-start.44 = (f32[6]{0:T(128)S(1)}, f32[6]{0:T(128)}, u32[]{:S(2)}) copy-start(f32[6]{0:T(128)} %constant.669) | copy-start | bytes 76
  38.5 16.8 %copy-start.99 = (f32[6]{0:T(128)S(1)}, f32[6]{0:T(128)}, u32[]{:S(2)}) copy-start(f32[6]{0:T(128)} %constant.434.clone) | copy-start | bytes 76
  38.5 16.8 %copy-start.102 = (f32[6]{0:T(128)S(1)}, f32[6]{0:T(128)}, u32[]{:S(2)}) copy-start(f32[6]{0:T(128)} %constant.432.clone) | copy-start | bytes 76
  38.5 16.8 %copy-start.105 = (f32[6]{0:T(128)S(1)}, f32[6]{0:T(128)}, u32[]{:S(2)}) copy-start(f32[6]{0:T(128)} %constant.433.clone) | copy-start | bytes 76
  60.8 23.3 %copy-start.17 = (f32[5,16,192]{2,1,0:T(8,128)}, f32[5,16,192]{2,1,0:T(8,128)S(1)}, u32[]{:S(2)}) copy-start(f32[5,16,192]{2,1,0:T(8,128)S(1)} %reshape.2129) | copy-start | bytes 184324
  63.4 8.4 %all-to-all-start.1 = ((bf16[3,4,1280]{2,0,1:T(4,128)(2,1)}), bf16[3,4,1280]{2,0,1:T(4,128)(2,1)S(1)}, u32[]{:S(2)}, u32[]{:S(2)}) async-start(bf16[3,4,1280]{2,0,1:T(4,128)(2,1)} %copy.1414), calls=%async_computation.1 | async-start | bytes 81920 | tf_op jit(solution)/shard_map/all_to_all | solution.py:180
  66.9 13.6 %copy-start.108 = (f32[1,16,192]{2,1,0:T(8,128)S(1)}, f32[1,16,192]{2,1,0:T(8,128)}, u32[]{:S(2)}) copy-start(f32[1,16,192]{2,1,0:T(8,128)} %get-tuple-element.361) | copy-start | bytes 36868
  71.9 11.7 %collective-permute-start.2 = (bf16[1,4,1280]{2,1,0:T(4,128)(2,1)S(1)}, bf16[1,4,1280]{2,1,0:T(4,128)(2,1)S(1)}, u32[]{:S(2)}, u32[]{:S(2)}) collective-permute-start(bf16[1,4,1280]{2,1,0:T(4,128)(2,1)S(1)} %copy.1583), channel_id=1, source_target_pairs={{0,28},{4,0},{8,4},{12,8},{16,12},{20,16},{24,20},{28,24},{1,29},{... | collective-permute-start | bytes 30728 | tf_op jit(solution)/shard_map/ppermute | solution.py:25
  76.6 7.0 %collective-permute-start.3 = (bf16[1,4,1280]{2,1,0:T(4,128)(2,1)S(1)}, bf16[1,4,1280]{2,1,0:T(4,128)(2,1)S(1)}, u32[]{:S(2)}, u32[]{:S(2)}) collective-permute-start(bf16[1,4,1280]{2,1,0:T(4,128)(2,1)S(1)} %copy.1585), channel_id=1, source_target_pairs={{0,4},{4,8},{8,12},{12,16},{16,20},{20,24},{24,28},{28,0},{1,5},{5... | collective-permute-start | bytes 30728 | tf_op jit(solution)/shard_map/ppermute | solution.py:25
  84.2 16.5 %copy-start.112 = (pred[192]{0:T(512)(128)(4,1)S(1)}, pred[192]{0:T(512)(128)(4,1)}, u32[]{:S(2)}) copy-start(pred[192]{0:T(512)(128)(4,1)} %broadcast_compare_fusion) | copy-start | bytes 580
  128.7 16.4 %copy-start.19 = (f32[5,16,192]{2,1,0:T(8,128)S(1)}, f32[5,16,192]{2,1,0:T(8,128)}, u32[]{:S(2)}) copy-start(f32[5,16,192]{2,1,0:T(8,128)} %copy-done.18) | copy-start | bytes 184324
  131.1 18.1 %copy-start.117 = (s32[192,1]{0,1:T(1,128)S(1)}, s32[192,1]{0,1:T(1,128)}, u32[]{:S(2)}) copy-start(s32[192,1]{0,1:T(1,128)} %compare_select_fusion.1) | copy-start | bytes 2308
  131.7 9.1 %collective-permute-start.4 = (bf16[1,4,1280]{2,1,0:T(4,128)(2,1)S(1)}, bf16[1,4,1280]{2,1,0:T(4,128)(2,1)S(1)}, u32[]{:S(2)}, u32[]{:S(2)}) collective-permute-start(bf16[1,4,1280]{2,1,0:T(4,128)(2,1)S(1)} %convert_element_type.92), channel_id=1, source_target_pairs={{0,4},{4,8},{8,12},{12,16},{16,20},{20,24},{24,28},{28,0},{1,5},{5... | collective-permute-start | bytes 30728 | tf_op jit(solution)/shard_map/ppermute | solution.py:25
  132.0 8.8 %collective-permute-start.5 = (bf16[1,4,1280]{2,1,0:T(4,128)(2,1)S(1)}, bf16[1,4,1280]{2,1,0:T(4,128)(2,1)S(1)}, u32[]{:S(2)}, u32[]{:S(2)}) collective-permute-start(bf16[1,4,1280]{2,1,0:T(4,128)(2,1)S(1)} %convert_element_type.93), channel_id=1, source_target_pairs={{0,28},{4,0},{8,4},{12,8},{16,12},{20,16},{24,20},{28,24},{1,29},{... | collective-permute-start | bytes 30728 | tf_op jit(solution)/shard_map/ppermute | solution.py:25
  141.5 7.4 %all-to-all-start.2 = ((bf16[3,4,1280]{2,0,1:T(4,128)(2,1)}), bf16[3,4,1280]{2,0,1:T(4,128)(2,1)S(1)}, u32[]{:S(2)}, u32[]{:S(2)}) async-start(bf16[3,4,1280]{2,0,1:T(4,128)(2,1)} %copy.1481), calls=%async_computation.2 | async-start | bytes 81920 | tf_op jit(solution)/shard_map/all_to_all | solution.py:184
  198.0 9.9 %collective-permute-start.6 = (bf16[1,4,1280]{2,1,0:T(4,128)(2,1)S(1)}, bf16[1,4,1280]{2,1,0:T(4,128)(2,1)S(1)}, u32[]{:S(2)}, u32[]{:S(2)}) collective-permute-start(bf16[1,4,1280]{2,1,0:T(4,128)(2,1)S(1)} %convert_element_type.94), channel_id=1, source_target_pairs={{0,4},{4,8},{8,12},{12,16},{16,20},{20,24},{24,28},{28,0},{1,5},{5... | collective-permute-start | bytes 30728 | tf_op jit(solution)/shard_map/ppermute | solution.py:25
  198.3 9.6 %collective-permute-start.7 = (bf16[1,4,1280]{2,1,0:T(4,128)(2,1)S(1)}, bf16[1,4,1280]{2,1,0:T(4,128)(2,1)S(1)}, u32[]{:S(2)}, u32[]{:S(2)}) collective-permute-start(bf16[1,4,1280]{2,1,0:T(4,128)(2,1)S(1)} %convert_element_type.95), channel_id=1, source_target_pairs={{0,28},{4,0},{8,4},{12,8},{16,12},{20,16},{24,20},{28,24},{1,29},{... | collective-permute-start | bytes 30728 | tf_op jit(solution)/shard_map/ppermute | solution.py:25
  208.6 7.2 %all-to-all-start.3 = ((bf16[3,4,1280]{2,0,1:T(4,128)(2,1)}), bf16[3,4,1280]{2,0,1:T(4,128)(2,1)S(1)}, u32[]{:S(2)}, u32[]{:S(2)}) async-start(bf16[3,4,1280]{2,0,1:T(4,128)(2,1)} %copy.1542), calls=%async_computation.3 | async-start | bytes 81920 | tf_op jit(solution)/shard_map/all_to_all | solution.py:184
  (114 other events, 778.5 us)
where the time goes:
time: 226 us; the launch traced here: 225 us
  local copies, waits for them, and re-layouts  108 us (48%)
  other arithmetic  71.7 us (32%)
  starting transfers between devices  33.9 us (15%)
  waiting for transfers between devices  5.91 us (3%)
  between operations  4.06 us (2%)
    scatter-add x2, other arithmetic, residual(): exterior = jnp.take(lookup.reshape(5, -1), gather_index, axis=1)  35.9 us
    gather x4, local copies, waits for them, and re-layouts, residual(): exterior = jnp.take(lookup.reshape(5, -1), gather_index, axis=1)  26 us
    another operation x94, local copies, waits for them, and re-layouts, flux_along(): return jnp.stack(components)  23 us
    ppermute x8, starting transfers between devices, from_behind(): return lax.ppermute(value, axis, pairs)  19.5 us
    scatter-add x2, other arithmetic, pack_sends(): picked = jnp.take(padded, slots, axis=2)  14.2 us
    reshape x6, local copies, waits for them, and re-layouts, residual(): exterior = jnp.take(lookup.reshape(5, -1), gather_index, axis=1)  9.15 us
    all_to_all x2, starting transfers between devices, sub_forward(): lax.all_to_all(buffer, 'sub', split_axis=1, concat_axis=1, tiled=True)  7.69 us
    all_to_all x2, starting transfers between devices, sub_backward(): lax.all_to_all(as_sent(buffer), 'sub', split_axis=1, concat_axis=1, tiled...  6.76 us
  transfers between devices with their start and end apart: 12, of which 2 were waited for; matrix products, arithmetic and copies ran while one was open for 19% of the time, Pallas kernels for 0%

commit v1 on v0

v1 whole, which is shorter than its diff:
```python
import jax
import jax.numpy as jnp
import numpy as np
from jax import lax
from jax.experimental import pallas as pl
from jax.experimental.pallas import tpu as pltpu
from jax.sharding import PartitionSpec as P

step_size = 0.02
mean_flow = 0.3
lift_factor = 12.0
LANES = 128
F32 = jnp.float32
BF16 = jnp.bfloat16


def derivative_table():
    points = np.array([-1.0, -1.0 / np.sqrt(5.0), 1.0 / np.sqrt(5.0), 1.0])
    products = np.array(
        [
            np.prod([points[target] - points[source] for source in range(4) if source != target])
            for target in range(4)
        ]
    )
    result = np.zeros((4, 4))
    for target in range(4):
        for source in range(4):
            if target != source:
                result[target, source] = products[target] / (
                    products[source] * (points[target] - points[source])
                )
        result[target, target] = -np.sum(result[target])
    return result.astype(np.float32)


def constants():
    nodes = np.arange(64).reshape(4, 4, 4)
    select = np.zeros((128, 6 * LANES), np.float32)
    for facet in range(6):
        layer = np.take(nodes, 3 * (facet % 2), axis=facet // 2).reshape(-1)
        for tile in range(3):
            for half in range(2):
                for m in range(16):
                    column = facet * LANES + tile * 32 + half * 16 + m
                    select[half * 64 + layer[m], column] = 1.0
    table = derivative_table()
    eye = np.eye(4, dtype=np.float32)
    along = [
        np.kron(np.kron(table, eye), eye),
        np.kron(np.kron(eye, table), eye),
        np.kron(np.kron(eye, eye), table),
    ]
    pair = np.eye(2, dtype=np.float32)
    forward = np.concatenate([np.kron(pair, -2.0 * d.T) for d in along], axis=0)
    backward = np.concatenate([np.kron(pair, -2.0 * d) for d in along], axis=1)

    def halves(x):
        high = x.astype(jnp.bfloat16)
        return high, (x - high.astype(np.float32)).astype(jnp.bfloat16)

    return (select.astype(jnp.bfloat16), select.T.astype(jnp.bfloat16), *halves(forward), *halves(backward))


def halves(x):
    high = x.astype(BF16)
    return high, (x - high.astype(F32)).astype(BF16)


def dot(x, y):
    return jnp.dot(x, y, preferred_element_type=F32)


def dot_split(x, w):
    high, low = halves(x)
    both = dot(jnp.concatenate([high, low], axis=0), w)
    return both[: x.shape[0]] + both[x.shape[0] :]


def dot_full(x, w_high, w_low):
    high, low = halves(x)
    both = dot(jnp.concatenate([high, low], axis=0), w_high)
    return both[: x.shape[0]] + both[x.shape[0] :] + dot(high, w_low)


def lanes_of(x, index):
    return jnp.take_along_axis(x, index, axis=1, mode="promise_in_bounds")


def iota(shape, axis):
    return lax.broadcasted_iota(jnp.int32, shape, axis)


def to_rows(x, elements):
    flat = x.reshape(320, elements)
    flat = jnp.concatenate([flat, jnp.zeros((64, elements), F32)], axis=0)
    return jnp.concatenate([flat[LANES * t : LANES * (t + 1)].T for t in range(3)], axis=0)


def from_rows(x, elements):
    return [x[elements * t : elements * (t + 1)].T for t in range(3)]


def traces(x, select, elements):
    wide = dot_split(x, select)
    block = iota((elements, LANES), 1) // 32
    parts = []
    for facet in range(6):
        cut = wide[:, LANES * facet : LANES * (facet + 1)]
        a, b, c = (cut[elements * t : elements * (t + 1)] for t in range(3))
        parts.append(jnp.where(block == 0, a, jnp.where(block == 1, b, c)))
    return jnp.concatenate(parts, axis=0)


def lift(x, select_t, elements):
    block = iota((elements, LANES), 1) // 32
    rows = []
    for t in range(3):
        rows.append(
            jnp.concatenate(
                [
                    jnp.where(block == t, x[elements * f : elements * (f + 1)], 0.0)
                    for f in range(6)
                ],
                axis=1,
            )
        )
    return dot_split(jnp.concatenate(rows, axis=0), select_t)


def volume_tables(elements):
    shape = (3 * elements, LANES)
    member = 2 * (iota(shape, 0) // elements) + iota(shape, 1) // 64
    return member


def spread(x, var, elements):
    tile, half = var // 2, var % 2
    part = x[elements * tile : elements * (tile + 1)]
    other = pltpu.roll(part, 64, 1)
    both = jnp.where(iota(part.shape, 1) // 64 == half, part, other)
    return jnp.concatenate([both] * 3, axis=0)


def volume(x, d_high, d_low, elements):
    member = volume_tables(elements)
    ends = jnp.where((member == 0) | (member == 4), 1.0, 0.0)
    pressure = spread(x, 4, elements)
    fluxes = []
    for a in range(3):
        speed = spread(x, 1 + a, elements)
        drift = mean_flow if a == 0 else 0.0
        fluxes.append(
            x * (speed + drift) + ends * speed + jnp.where(member == 1 + a, pressure, 0.0)
        )
    return dot_full(jnp.concatenate(fluxes, axis=1), d_high, d_low)


def volume_back(x, slopes, elements):
    member = volume_tables(elements)
    ends = jnp.where((member == 0) | (member == 4), 1.0, 0.0)
    total = None
    for a in range(3):
        g = slopes[:, LANES * a : LANES * (a + 1)]
        drift = mean_flow if a == 0 else 0.0
        speed = spread(x, 1 + a, elements)
        product = (x + ends) * g
        summed = product[:elements] + product[elements : 2 * elements] + product[2 * elements :]
        summed = summed + pltpu.roll(summed, 64, 1)
        summed = jnp.concatenate([summed] * 3, axis=0)
        term = (speed + drift) * g + jnp.where(member == 1 + a, summed, 0.0)
        term = term + jnp.where(member == 4, spread(g, 1 + a, elements), 0.0)
        total = term if total is None else total + term
    return total


class Faces:
    def __init__(self, elements):
        shape = (6 * elements, LANES)
        lane = iota(shape, 1)
        facet = iota(shape, 0) // elements
        self.node = lane % 16
        self.member = lane // 16
        self.axis = facet // 2
        self.sign = (2 * (facet % 2) - 1).astype(F32)
        self.drift = jnp.where(self.axis == 0, mean_flow, 0.0)
        self.normal = self.member == 1 + self.axis
        self.ends = jnp.where((self.member == 0) | (self.member == 4), 1.0, 0.0)
        self.mirror = jnp.where(self.normal, -1.0, 1.0)
        self.at_speed = (1 + self.axis) * 16 + self.node
        self.at_pressure = 64 + self.node

    def flux(self, q):
        speed = lanes_of(q, self.at_speed)
        pressure = lanes_of(q, self.at_pressure)
        return self.sign * (
            q * (speed + self.drift) + self.ends * speed + jnp.where(self.normal, pressure, 0.0)
        )

    def back(self, q, w, axis=None):
        if axis is None:
            at, drift, normal = self.at_speed, self.drift, self.normal
        else:
            at = (1 + axis) * 16 + self.node
            drift = mean_flow if axis == 0 else 0.0
            normal = self.member == 1 + axis
        product = (q + self.ends) * w
        for shift in (64, 32, 16):
            product = product + pltpu.roll(product, shift, 1)
        term = (lanes_of(q, at) + drift) * w + jnp.where(normal, product, 0.0)
        return term + jnp.where(self.member == 4, lanes_of(w, at), 0.0)

    def jump(self, inner, outer):
        return 0.5 * (self.flux(inner) - self.flux(outer)) + (outer - inner)


def column(values, elements):
    lead, width = values.shape
    x = values.astype(F32)
    x = jnp.concatenate([x, jnp.zeros((8 - lead, width), F32)], axis=0)
    x = x.T
    return jnp.concatenate([x[:, f : f + 1] for f in range(lead)], axis=0).astype(jnp.int32)


def one_hot(flags):
    return jnp.where(flags, 1.0, 0.0).astype(BF16)


def program(state, final, slots, ext_row, ext, perm, mats, net):
    select, select_t, d_high, d_low, b_high, b_low = (m[...] for m in mats)
    elements = state.shape[2]
    n_faces = 6 * elements
    n_slots = slots.shape[1]
    faces = Faces(elements)

    net.greet()
    x0 = to_rows(state, elements)
    t0 = traces(x0, select, elements)
    slot_column = column(slots, elements)
    pick = one_hot(slot_column == iota((n_slots, n_faces), 1))
    net.send(0, lambda: dot(pick, t0.astype(BF16)).astype(BF16))

    ext_column = column(ext, elements)
    perm_column = column(perm, elements) + jnp.zeros((n_faces, LANES), jnp.int32)
    wall = ext_column + jnp.zeros((n_faces, LANES), jnp.int32) == n_faces + n_slots
    flip_r = (perm_column & 1) != 0
    flip_s = (perm_column & 2) != 0
    swap = (perm_column & 4) != 0
    base = faces.member * 16
    r, s = faces.node // 4, faces.node % 4
    r_new = jnp.where(flip_r, 3 - r, r)
    s_new = jnp.where(flip_s, 3 - s, s)
    orient = base + jnp.where(swap, 4 * s_new + r_new, 4 * r_new + s_new)
    r_old = jnp.where(swap, s, r)
    s_old = jnp.where(swap, r, s)
    r_old = jnp.where(flip_r, 3 - r_old, r_old)
    s_old = jnp.where(flip_s, 3 - s_old, s_old)
    unorient = base + 4 * r_old + s_old

    to_local = one_hot(ext_row == iota((n_faces, n_faces), 0))
    to_slots = one_hot(ext_row - n_faces == iota((n_slots, n_faces), 0))
    unpick = one_hot(slots == iota((n_faces, n_slots), 0))

    w = to_rows(final, elements)
    w_jump = lift_factor * traces(w, select, elements)
    w_turned = lanes_of(jnp.where(wall, 0.0, w_jump), unorient)

    def by_axis(x):
        signed = faces.sign * x
        return jnp.concatenate(
            [jnp.where(faces.axis == a, signed, 0.0) for a in range(3)] + [x], axis=1
        )

    cot = by_axis(w_turned)
    cot_high, cot_low = halves(cot)
    net.send(1, lambda: dot(to_slots, cot_high).astype(BF16))

    from_local = one_hot(ext_column == iota((n_faces, n_faces), 1))
    from_slots = one_hot(ext_column - n_faces == iota((n_faces, n_slots), 1))

    def outer_local(t):
        both = dot(from_local, jnp.concatenate(halves(t), axis=1))
        return both[:, :LANES] + both[:, LANES:]

    def outer(t, local, received):
        e = lanes_of(local + dot(from_slots, received), orient)
        return jnp.where(wall, t * faces.mirror, e)

    def jump(t, e):
        return faces.jump(t, e)

    local0 = outer_local(t0)
    rate0 = volume(x0, d_high, d_low, elements)
    cot_local = dot(to_local, cot_high) + dot(to_local, cot_low) - by_axis(w_jump)
    slopes = dot_full(w, b_high, b_low)

    e0 = outer(t0, local0, net.wait(0))
    x1 = x0 + step_size * (rate0 + lift_factor * lift(jump(t0, e0), select_t, elements))
    t1 = traces(x1, select, elements)
    net.send(2, lambda: dot(pick, t1.astype(BF16)).astype(BF16))

    back1 = volume_back(x1, slopes, elements)
    wall_out = w_jump - 0.5 * faces.sign * faces.back(t1 * faces.mirror, w_jump)
    t_bar = jnp.where(wall, faces.mirror * wall_out, 0.0)
    cot_all = cot_local + dot(unpick, net.wait(1))
    t_bar = t_bar + cot_all[:, 3 * LANES :]
    for a in range(3):
        t_bar = t_bar - 0.5 * faces.back(t1, cot_all[:, LANES * a : LANES * (a + 1)], a)
    w1 = 0.5 * w + 0.5 * step_size * (back1 + lift(t_bar, select_t, elements))

    w1_jump = lift_factor * traces(w1, select, elements)
    out_bar = w1_jump - 0.5 * faces.sign * faces.back(e0, w1_jump)
    turned = lanes_of(jnp.where(wall, 0.0, out_bar), unorient)
    turned_high, turned_low = halves(turned)
    net.send(3, lambda: dot(to_slots, turned_high).astype(BF16))

    in_bar = 0.5 * faces.sign * faces.back(t0, w1_jump) - w1_jump
    in_bar = in_bar + jnp.where(wall, faces.mirror * out_bar, 0.0)
    in_bar = in_bar + dot(to_local, turned_high) + dot(to_local, turned_low)
    slopes1 = dot_full(w1, b_high, b_low)
    back0 = volume_back(x0, slopes1, elements)
    start = 0.5 * w + w1 + step_size * back0

    local1 = outer_local(t1)
    rate1 = volume(x1, d_high, d_low, elements)
    e1 = outer(t1, local1, net.wait(2))
    rate1 = rate1 + lift_factor * lift(jump(t1, e1), select_t, elements)
    net.output(0, from_rows(0.5 * x0 + 0.5 * (x1 + step_size * rate1), elements))

    in_bar = in_bar + dot(unpick, net.wait(3))
    start = start + step_size * lift(in_bar, select_t, elements)
    net.output(1, from_rows(start, elements))


class Net:
    def __init__(self, n_dom, n_sub, outs, send_bufs, recv_bufs, send_sem, recv_sem):
        self.n_dom, self.n_sub = n_dom, n_sub
        self.dom, self.sub = lax.axis_index("dom"), lax.axis_index("sub")
        self.outs = outs
        self.send_bufs, self.recv_bufs = send_bufs, recv_bufs
        self.send_sem, self.recv_sem = send_sem, recv_sem
        self.greeted = False

    def partners(self):
        for group in (0, 2, 1):
            for j in range(self.n_sub):
                if group != 1 or j != 0:
                    yield group, lax.rem(self.sub + j, self.n_sub)

    def neighbour(self, steps):
        return lax.rem(self.dom + steps + self.n_dom, self.n_dom)

    def greet(self):
        barrier = pltpu.get_barrier_semaphore()
        for group, other in self.partners():
            pl.semaphore_signal(
                barrier,
                inc=1,
                device_id=(self.neighbour(group - 1), other),
                device_id_type=pl.DeviceIdType.MESH,
            )

    def copies(self, phase):
        source, target = self.send_bufs[phase], self.recv_bufs[phase]
        size = source.shape[0] // (3 * self.n_sub)
        way = 1 if phase % 2 == 0 else -1
        for group, other in self.partners():
            there = pl.multiple_of((group * self.n_sub + other) * size, size)
            here = pl.multiple_of((group * self.n_sub + self.sub) * size, size)
            yield pltpu.make_async_remote_copy(
                src_ref=source.at[pl.ds(there, size)],
                dst_ref=target.at[pl.ds(here, size)],
                send_sem=self.send_sem.at[phase, group * self.n_sub + other],
                recv_sem=self.recv_sem.at[phase, group * self.n_sub + self.sub],
                device_id=(self.neighbour(way * (group - 1)), other),
                device_id_type=pl.DeviceIdType.MESH,
            )

    def send(self, phase, make):
        source, target = self.send_bufs[phase], self.recv_bufs[phase]
        source[...] = make()
        if not self.greeted:
            pl.semaphore_wait(pltpu.get_barrier_semaphore(), 3 * self.n_sub - 1)
            self.greeted = True
        for copy in self.copies(phase):
            copy.start()
        size = source.shape[0] // (3 * self.n_sub)
        own = pl.ds(pl.multiple_of((self.n_sub + self.sub) * size, size), size)
        target[own] = source[own]

    def wait(self, phase):
        source, target = self.send_bufs[phase], self.recv_bufs[phase]
        size = source.shape[0] // (3 * self.n_sub)
        for group, other in self.partners():
            rows = pl.ds(pl.multiple_of((group * self.n_sub + other) * size, size), size)
            index = group * self.n_sub + other
            pltpu.make_async_remote_copy(
                src_ref=source.at[rows],
                dst_ref=target.at[rows],
                send_sem=self.send_sem.at[phase, index],
                recv_sem=self.recv_sem.at[phase, index],
                device_id=(self.neighbour(group - 1), other),
                device_id_type=pl.DeviceIdType.MESH,
            ).wait_recv()
        return target[...]

    def finish(self):
        for phase in range(4):
            for copy in self.copies(phase):
                copy.wait_send()

    def output(self, which, parts):
        for t in range(3):
            for half in range(2):
                if 2 * t + half < 5:
                    self.outs[which][2 * t + half] = parts[t][64 * half : 64 * (half + 1)]


def kernel(n_dom, n_sub, *refs):
    state, final, slots, ext_row, ext, perm = refs[:6]
    mats = refs[6:12]
    outs = refs[12:14]
    send_bufs, recv_bufs = refs[14:18], refs[18:22]
    net = Net(n_dom, n_sub, outs, send_bufs, recv_bufs, refs[22], refs[23])
    program(state[...], final[...], slots[...], ext_row[...], ext[...], perm[...], mats, net)
    net.finish()


def solution(mesh):
    n_dom, n_sub = mesh.shape["dom"], mesh.shape["sub"]
    mats = constants()

    def shards(state, final, send_slot, ext_index, ext_perm):
        n_slots = send_slot.shape[1]
        widths = (LANES, 4 * LANES, LANES, LANES)
        vmem = pl.BlockSpec(memory_space=pltpu.VMEM)
        buffers = [pltpu.VMEM((n_slots, width), BF16) for width in widths]
        result = jax.ShapeDtypeStruct(state.shape, F32)
        return pl.pallas_call(
            lambda *refs: kernel(n_dom, n_sub, *refs),
            out_shape=(result, result),
            in_specs=[vmem] * 12,
            out_specs=(vmem, vmem),
            scratch_shapes=buffers
            + buffers
            + [
                pltpu.SemaphoreType.DMA((4, 3 * n_sub)),
                pltpu.SemaphoreType.DMA((4, 3 * n_sub)),
            ],
            compiler_params=pltpu.CompilerParams(
                collective_id=0, has_side_effects=True, vmem_limit_bytes=32 * 1024 * 1024
            ),
        )(
            state,
            final,
            send_slot,
            ext_index.reshape(1, -1),
            ext_index,
            ext_perm,
            *[jnp.asarray(m) for m in mats],
        )

    return jax.shard_map(
        shards,
        mesh=mesh,
        in_specs=(
            P(None, None, ("dom", "sub")),
            P(None, None, ("dom", "sub")),
            P(("dom", "sub"), None),
            P(None, ("dom", "sub")),
            P(None, ("dom", "sub")),
        ),
        out_specs=(P(None, None, ("dom", "sub")), P(None, None, ("dom", "sub"))),
        check_vma=False,
    )
```

time: 226 us -> 29.7 us (0.13)
  local copies, waits for them, and re-layouts: 108 us -> 7.77 us
  other arithmetic: 71.7 us -> 0 us
  starting transfers between devices: 33.9 us -> 0 us
  Pallas kernels: 0 us -> 20.8 us
  waiting for transfers between devices: 5.91 us -> 0 us
  between operations: 4.06 us -> 0.72 us
    scatter-add x8 -> x0, other arithmetic: 50.2 us -> none  [the longest x2 35.9 us: residual(): exterior = jnp.take(lookup.reshape(5, -1), gather_index, axis=1)]
    another operation x123 -> x0, local copies, waits for them, and re-layouts: 28.2 us -> none  [the longest x94 23 us: flux_along(): return jnp.stack(components)]
    gather x12 -> x0, local copies, waits for them, and re-layouts: 27.8 us -> none  [the longest x4 26 us: residual(): exterior = jnp.take(lookup.reshape(5, -1), gather_index, axis=1)]
    pallas_call x0 -> x1, Pallas kernels: none -> 20.8 us  [shards(): pl.pallas_call(lambda *refs: kernel(n_dom, n_sub, *refs), out_shape=(resu...]
    ppermute x8 -> x0, starting transfers between devices: 19.5 us -> none  [from_behind(): return lax.ppermute(value, axis, pairs)]
    all_to_all x4 -> x0, starting transfers between devices: 14.4 us -> none  [the longest x2 7.69 us: sub_forward(): lax.all_to_all(buffer, 'sub', split_axis=1, concat_axis=1, tiled=True)]
    reshape x21 -> x1, local copies, waits for them, and re-layouts: 12.7 us -> 0.82 us  [shards(): ext_index.reshape(1, -1)]
    scatter-add x10 -> x0, local copies, waits for them, and re-layouts: 10.9 us -> none  [the longest x2 4.47 us: residual(): exterior = jnp.take(lookup.reshape(5, -1), gather_index, axis=1)]
  transfers between devices with their start and end apart: 12 -> 0, of which waited for: 2 -> 0; matrix products, arithmetic and copies ran while one was open for 19% -> 0% of each run, Pallas kernels for 0% -> 0%
where the time goes in v1:
time: 29.7 us; the launch traced here: 29.3 us
  Pallas kernels  20.8 us (70%)
  local copies, waits for them, and re-layouts  7.77 us (26%)
  between operations  0.72 us (2%)
    pallas_call x1, Pallas kernels, shards(): pl.pallas_call(lambda *refs: kernel(n_dom, n_sub, *refs), out_shape=(resu...  20.8 us
    unnamed x20, local copies, waits for them, and re-layouts  5.46 us
    pallas_call x2, local copies, waits for them, and re-layouts, shards(): pl.pallas_call(lambda *refs: kernel(n_dom, n_sub, *refs), out_shape=(resu...  1.49 us
    reshape x1, local copies, waits for them, and re-layouts, shards(): ext_index.reshape(1, -1)  0.82 us

profile of v1, /device:TPU:0, one launch (start us, length us, event | category | flops | bytes accessed | tf_op | source)
XLA Modules:
  0.0 29.3 jit_solution(8846032100554756119)
XLA Ops:
  0.6 0.0 copy-start.6
  0.6 0.0 copy-start.8
  0.6 0.8 %reshape.7.refs_3_ = s32[1,192]{1,0:T(1,128)S(1)} reshape(s32[6,32]{1,0:T(8,128)} %refs_4_.1) | data formatting | bytes 1536 | tf_op jit(solution)/shard_map/reshape | solution.py:456
  1.5 0.0 copy-start
  1.5 0.0 copy-start.1
  1.5 1.0 %copy.13.refs_0_ = f32[5,64,32]{2,1,0:T(8,128)S(1)} copy(f32[5,64,32]{1,2,0:T(8,128)} %param.11) | data formatting | bytes 81920 | tf_op args[0]
  2.5 0.0 copy-start.2
  2.5 1.0 %copy.14.refs_1_ = f32[5,64,32]{2,1,0:T(8,128)S(1)} copy(f32[5,64,32]{1,2,0:T(8,128)} %param.12) | data formatting | bytes 81920 | tf_op args[1]
  3.6 0.0 copy-done.6
  3.6 0.0 copy-done.8
  3.6 0.0 copy-done
  3.6 0.0 copy-done.1
  3.6 0.0 copy-done.2
  3.6 0.0 copy-start.3
  3.6 0.9 %copy-done.3 = bf16[128,384]{1,0:T(8,128)(2,1)S(1)} copy-done((bf16[128,384]{1,0:T(8,128)(2,1)S(1)}, bf16[128,384]{1,0:T(8,128)(2,1)}, u32[]{:S(2)}) %copy-start.3) | copy-done | bytes 98328
  4.5 0.0 copy-start.4
  4.5 0.9 %copy-done.4 = bf16[384,128]{1,0:T(8,128)(2,1)S(1)} copy-done((bf16[384,128]{1,0:T(8,128)(2,1)S(1)}, bf16[384,128]{1,0:T(8,128)(2,1)}, u32[]{:S(2)}) %copy-start.4) | copy-done | bytes 98328
  5.4 0.0 copy-start.5
  5.4 0.9 %copy-done.5 = bf16[384,128]{1,0:T(8,128)(2,1)S(1)} copy-done((bf16[384,128]{1,0:T(8,128)(2,1)S(1)}, bf16[384,128]{1,0:T(8,128)(2,1)}, u32[]{:S(2)}) %copy-start.5) | copy-done | bytes 98328
  6.3 0.0 copy-start.7
  6.3 0.7 %copy-done.7 = s32[6,32]{1,0:T(8,128)S(1)} copy-done((s32[6,32]{1,0:T(8,128)S(1)}, s32[6,32]{1,0:T(8,128)}, u32[]{:S(2)}) %copy-start.7) | copy-done | bytes 792
  7.0 20.8 %shard_map.122 = (f32[5,64,32]{2,1,0:T(8,128)S(1)}, f32[5,64,32]{2,1,0:T(8,128)S(1)}) custom-call(f32[5,64,32]{2,1,0:T(8,128)S(1)} %copy.13.refs_0_, f32[5,64,32]{2,1,0:T(8,128)S(1)} %copy.14.refs_1_, s32[1,192]{1,0:T(1,128)S(1)} %copy-done.8, s32[1,192]{1,0:T(1,128)S(1)} %reshape.7.refs_3_, s32[6,32]{1,0:T(8,128)S(1)} %copy-done.6, s32[6,32]{1,0:T(8,128)S(1)} %copy-done.7, ...), custom_call_target="tpu_custom_call" | custom-call | tf_op jit(solution)/shard_map/pallas_call | solution.py:438
  27.8 0.7 %copy.15 = f32[5,64,32]{1,2,0:T(8,128)} copy(f32[5,64,32]{2,1,0:T(8,128)S(1)} %get-tuple-element.2) | data formatting | bytes 81920 | tf_op jit(solution)/shard_map/pallas_call | solution.py:438
  28.6 0.7 %copy.16 = f32[5,64,32]{1,2,0:T(8,128)} copy(f32[5,64,32]{2,1,0:T(8,128)S(1)} %get-tuple-element.3) | data formatting | bytes 81920 | tf_op jit(solution)/shard_map/pallas_call | solution.py:438
Async XLA Ops:
  0.6 2.9 %copy-start.6 = (s32[6,32]{1,0:T(8,128)S(1)}, s32[6,32]{1,0:T(8,128)}, u32[]{:S(2)}) copy-start(s32[6,32]{1,0:T(8,128)} %refs_4_.1) | copy-start | bytes 2308
  0.6 2.9 %copy-start.8 = (s32[1,192]{1,0:T(1,128)S(1)}, s32[1,192]{1,0:T(1,128)}, u32[]{:S(2)}) copy-start(s32[1,192]{1,0:T(1,128)} %refs_2_.1) | copy-start | bytes 2308
  1.5 2.1 %copy-start = (bf16[768,128]{1,0:T(8,128)(2,1)S(1)}, bf16[768,128]{1,0:T(8,128)(2,1)}, u32[]{:S(2)}) copy-start(bf16[768,128]{1,0:T(8,128)(2,1)} %constant.13.clone.refs_7_) | copy-start | bytes 589828
  1.5 2.1 %copy-start.1 = (bf16[128,768]{1,0:T(8,128)(2,1)S(1)}, bf16[128,768]{1,0:T(8,128)(2,1)}, u32[]{:S(2)}) copy-start(bf16[128,768]{1,0:T(8,128)(2,1)} %constant.12.clone.refs_6_) | copy-start | bytes 589828
  2.5 1.1 %copy-start.2 = (bf16[128,384]{1,0:T(8,128)(2,1)S(1)}, bf16[128,384]{1,0:T(8,128)(2,1)}, u32[]{:S(2)}) copy-start(bf16[128,384]{1,0:T(8,128)(2,1)} %constant.17.clone.refs_11_) | copy-start | bytes 294916
  3.6 0.9 %copy-start.3 = (bf16[128,384]{1,0:T(8,128)(2,1)S(1)}, bf16[128,384]{1,0:T(8,128)(2,1)}, u32[]{:S(2)}) copy-start(bf16[128,384]{1,0:T(8,128)(2,1)} %constant.16.clone.refs_10_) | copy-start | bytes 294916
  4.5 0.9 %copy-start.4 = (bf16[384,128]{1,0:T(8,128)(2,1)S(1)}, bf16[384,128]{1,0:T(8,128)(2,1)}, u32[]{:S(2)}) copy-start(bf16[384,128]{1,0:T(8,128)(2,1)} %constant.15.clone.refs_9_) | copy-start | bytes 294916
  5.4 0.9 %copy-start.5 = (bf16[384,128]{1,0:T(8,128)(2,1)S(1)}, bf16[384,128]{1,0:T(8,128)(2,1)}, u32[]{:S(2)}) copy-start(bf16[384,128]{1,0:T(8,128)(2,1)} %constant.14.clone.refs_8_) | copy-start | bytes 294916
  6.3 0.7 %copy-start.7 = (s32[6,32]{1,0:T(8,128)S(1)}, s32[6,32]{1,0:T(8,128)}, u32[]{:S(2)}) copy-start(s32[6,32]{1,0:T(8,128)} %refs_5_.1) | copy-start | bytes 2308

commit v2 on v1

--- a/solution.py
+++ b/solution.py
@@ -34,15 +34,6 @@
 
 
 def constants():
-    nodes = np.arange(64).reshape(4, 4, 4)
-    select = np.zeros((128, 6 * LANES), np.float32)
-    for facet in range(6):
-        layer = np.take(nodes, 3 * (facet % 2), axis=facet // 2).reshape(-1)
-        for tile in range(3):
-            for half in range(2):
-                for m in range(16):
-                    column = facet * LANES + tile * 32 + half * 16 + m
-                    select[half * 64 + layer[m], column] = 1.0
     table = derivative_table()
     eye = np.eye(4, dtype=np.float32)
     along = [
@@ -51,14 +42,12 @@
         np.kron(np.kron(eye, eye), table),
     ]
     pair = np.eye(2, dtype=np.float32)
-    forward = np.concatenate([np.kron(pair, -2.0 * d.T) for d in along], axis=0)
-    backward = np.concatenate([np.kron(pair, -2.0 * d) for d in along], axis=1)
-
-    def halves(x):
-        high = x.astype(jnp.bfloat16)
-        return high, (x - high.astype(np.float32)).astype(jnp.bfloat16)
-
-    return (select.astype(jnp.bfloat16), select.T.astype(jnp.bfloat16), *halves(forward), *halves(backward))
+    parts = []
+    for d in ([x.T for x in along], along):
+        full = np.concatenate([np.kron(pair, -2.0 * x) for x in d], axis=0)
+        high = full.astype(jnp.bfloat16)
+        parts += [high, (full - high.astype(np.float32)).astype(jnp.bfloat16)]
+    return np.concatenate(parts, axis=0)
 
 
 def halves(x):
@@ -68,12 +57,6 @@
 
 def dot(x, y):
     return jnp.dot(x, y, preferred_element_type=F32)
-
-
-def dot_split(x, w):
-    high, low = halves(x)
-    both = dot(jnp.concatenate([high, low], axis=0), w)
-    return both[: x.shape[0]] + both[x.shape[0] :]
 
 
 def dot_full(x, w_high, w_low):
@@ -90,41 +73,61 @@
     return lax.broadcasted_iota(jnp.int32, shape, axis)
 
 
-def to_rows(x, elements):
-    flat = x.reshape(320, elements)
-    flat = jnp.concatenate([flat, jnp.zeros((64, elements), F32)], axis=0)
-    return jnp.concatenate([flat[LANES * t : LANES * (t + 1)].T for t in range(3)], axis=0)
-
-
-def from_rows(x, elements):
-    return [x[elements * t : elements * (t + 1)].T for t in range(3)]
-
-
-def traces(x, select, elements):
-    wide = dot_split(x, select)
-    block = iota((elements, LANES), 1) // 32
+def dot_stacked(x, w_high, w_low):
+    high, low = halves(x)
+    wide = jnp.concatenate(
+        [
+            jnp.concatenate([high, high], axis=1),
+            jnp.concatenate([low, jnp.zeros_like(low)], axis=1),
+        ],
+        axis=0,
+    )
+    both = dot(wide, jnp.concatenate([w_high, w_low], axis=0))
+    return both[: x.shape[0]] + both[x.shape[0] :]
+
+
+def to_rows(x):
+    pairs = [jnp.concatenate([x[2 * t], x[2 * t + 1]], axis=1) for t in range(2)]
+    pairs.append(jnp.concatenate([x[4], jnp.zeros_like(x[4])], axis=1))
+    return jnp.concatenate(pairs, axis=0)
+
+
+def traces(x, elements):
+    lane = iota((elements, LANES), 1)
+    block = lane // 32
+    m = lane % 16
     parts = []
     for facet in range(6):
-        cut = wide[:, LANES * facet : LANES * (facet + 1)]
-        a, b, c = (cut[elements * t : elements * (t + 1)] for t in range(3))
+        layer = 3 * (facet % 2)
+        if facet < 2:
+            node = 16 * layer + m
+        elif facet < 4:
+            node = 16 * (m // 4) + 4 * layer + m % 4
+        else:
+            node = 4 * m + layer
+        at = jnp.where(block == 3, 64, 64 * (lane // 16 % 2) + node)
+        a, b, c = (lanes_of(x[elements * t : elements * (t + 1)], at) for t in range(3))
         parts.append(jnp.where(block == 0, a, jnp.where(block == 1, b, c)))
     return jnp.concatenate(parts, axis=0)
 
 
-def lift(x, select_t, elements):
-    block = iota((elements, LANES), 1) // 32
+def lift(x, elements):
+    lane = iota((elements, LANES), 1)
+    half, node = lane // 64, lane % 64
+    i, j, k = node // 16, node // 4 % 4, node % 4
     rows = []
     for t in range(3):
-        rows.append(
-            jnp.concatenate(
-                [
-                    jnp.where(block == t, x[elements * f : elements * (f + 1)], 0.0)
-                    for f in range(6)
-                ],
-                axis=1,
+        base = (2 * t + half) * 16
+        total = None
+        for axis, (along, m) in enumerate(((i, node % 16), (j, 4 * i + k), (k, 4 * i + j))):
+            low, high = (
+                lanes_of(x[elements * f : elements * (f + 1)], base + m)
+                for f in (2 * axis, 2 * axis + 1)
             )
-        )
-    return dot_split(jnp.concatenate(rows, axis=0), select_t)
+            term = jnp.where(along == 0, low, jnp.where(along == 3, high, 0.0))
+            total = term if total is None else total + term
+        rows.append(total)
+    return jnp.concatenate(rows, axis=0)
 
 
 def volume_tables(elements):
@@ -213,7 +216,7 @@
         return 0.5 * (self.flux(inner) - self.flux(outer)) + (outer - inner)
 
 
-def column(values, elements):
+def column(values):
     lead, width = values.shape
     x = values.astype(F32)
     x = jnp.concatenate([x, jnp.zeros((8 - lead, width), F32)], axis=0)
@@ -225,22 +228,24 @@
     return jnp.where(flags, 1.0, 0.0).astype(BF16)
 
 
-def program(state, final, slots, ext_row, ext, perm, mats, net):
-    select, select_t, d_high, d_low, b_high, b_low = (m[...] for m in mats)
-    elements = state.shape[2]
+def program(net):
+    net.greet()
+    state = net.load(0)
+    elements = state.shape[1]
     n_faces = 6 * elements
+    faces = Faces(elements)
+    x0 = to_rows(state)
+    t0 = traces(x0, elements)
+    slots = net.load(1)
     n_slots = slots.shape[1]
-    faces = Faces(elements)
-
-    net.greet()
-    x0 = to_rows(state, elements)
-    t0 = traces(x0, select, elements)
-    slot_column = column(slots, elements)
+    slot_column = column(slots)
     pick = one_hot(slot_column == iota((n_slots, n_faces), 1))
     net.send(0, lambda: dot(pick, t0.astype(BF16)).astype(BF16))
 
-    ext_column = column(ext, elements)
-    perm_column = column(perm, elements) + jnp.zeros((n_faces, LANES), jnp.int32)
+    ext = net.load(2)
+    ext_row = jnp.concatenate([ext[f : f + 1] for f in range(6)], axis=1)
+    ext_column = column(ext)
+    perm_column = column(net.load(3)) + jnp.zeros((n_faces, LANES), jnp.int32)
     wall = ext_column + jnp.zeros((n_faces, LANES), jnp.int32) == n_faces + n_slots
     flip_r = (perm_column & 1) != 0
     flip_s = (perm_column & 2) != 0
@@ -260,18 +265,29 @@
     to_slots = one_hot(ext_row - n_faces == iota((n_slots, n_faces), 0))
     unpick = one_hot(slots == iota((n_faces, n_slots), 0))
 
-    w = to_rows(final, elements)
-    w_jump = lift_factor * traces(w, select, elements)
+    w = to_rows(net.load(4))
+    w_jump = lift_factor * traces(w, elements)
     w_turned = lanes_of(jnp.where(wall, 0.0, w_jump), unorient)
+
+    spare = faces.member >= 5
 
     def by_axis(x):
         signed = faces.sign * x
-        return jnp.concatenate(
-            [jnp.where(faces.axis == a, signed, 0.0) for a in range(3)] + [x], axis=1
+        tiles = [jnp.where(faces.axis == a, signed, 0.0) for a in range(3)]
+        tiles[0] = jnp.where(spare, pltpu.roll(x, 80, 1), tiles[0])
+        tiles[1] = jnp.where(spare, pltpu.roll(x, 32, 1), tiles[1])
+        return jnp.concatenate(tiles, axis=1)
+
+    def unpacked(x):
+        tiles = [x[:, LANES * a : LANES * (a + 1)] for a in range(3)]
+        plain = jnp.where(
+            faces.member < 3,
+            pltpu.roll(tiles[0], 48, 1),
+            jnp.where(spare, 0.0, pltpu.roll(tiles[1], 96, 1)),
         )
-
-    cot = by_axis(w_turned)
-    cot_high, cot_low = halves(cot)
+        return [jnp.where(spare, 0.0, tiles[0]), jnp.where(spare, 0.0, tiles[1]), tiles[2], plain]
+
+    cot_high, cot_low = halves(by_axis(w_turned))
     net.send(1, lambda: dot(to_slots, cot_high).astype(BF16))
 
     from_local = one_hot(ext_column == iota((n_faces, n_faces), 1))
@@ -289,25 +305,32 @@
         return faces.jump(t, e)
 
     local0 = outer_local(t0)
+    size = 3 * LANES
+    mats = net.load(5)
+    d_high, d_low = mats[:size], mats[size : 2 * size]
+    b_high, b_low = (
+        jnp.concatenate([mats[at + LANES * a : at + LANES * (a + 1)] for a in range(3)], axis=1)
+        for at in (2 * size, 3 * size)
+    )
     rate0 = volume(x0, d_high, d_low, elements)
     cot_local = dot(to_local, cot_high) + dot(to_local, cot_low) - by_axis(w_jump)
-    slopes = dot_full(w, b_high, b_low)
+    slopes = dot_stacked(w, b_high, b_low)
 
     e0 = outer(t0, local0, net.wait(0))
-    x1 = x0 + step_size * (rate0 + lift_factor * lift(jump(t0, e0), select_t, elements))
-    t1 = traces(x1, select, elements)
+    x1 = x0 + step_size * (rate0 + lift_factor * lift(jump(t0, e0), elements))
+    t1 = traces(x1, elements)
     net.send(2, lambda: dot(pick, t1.astype(BF16)).astype(BF16))
 
     back1 = volume_back(x1, slopes, elements)
     wall_out = w_jump - 0.5 * faces.sign * faces.back(t1 * faces.mirror, w_jump)
     t_bar = jnp.where(wall, faces.mirror * wall_out, 0.0)
-    cot_all = cot_local + dot(unpick, net.wait(1))
-    t_bar = t_bar + cot_all[:, 3 * LANES :]
+    cot_all = unpacked(cot_local + dot(unpick, net.wait(1)))
+    t_bar = t_bar + cot_all[3]
     for a in range(3):
-        t_bar = t_bar - 0.5 * faces.back(t1, cot_all[:, LANES * a : LANES * (a + 1)], a)
-    w1 = 0.5 * w + 0.5 * step_size * (back1 + lift(t_bar, select_t, elements))
-
-    w1_jump = lift_factor * traces(w1, select, elements)
+        t_bar = t_bar - 0.5 * faces.back(t1, cot_all[a], a)
+    w1 = 0.5 * w + 0.5 * step_size * (back1 + lift(t_bar, elements))
+
+    w1_jump = lift_factor * traces(w1, elements)
     out_bar = w1_jump - 0.5 * faces.sign * faces.back(e0, w1_jump)
     turned = lanes_of(jnp.where(wall, 0.0, out_bar), unorient)
     turned_high, turned_low = halves(turned)
@@ -316,29 +339,40 @@
     in_bar = 0.5 * faces.sign * faces.back(t0, w1_jump) - w1_jump
     in_bar = in_bar + jnp.where(wall, faces.mirror * out_bar, 0.0)
     in_bar = in_bar + dot(to_local, turned_high) + dot(to_local, turned_low)
-    slopes1 = dot_full(w1, b_high, b_low)
+    slopes1 = dot_stacked(w1, b_high, b_low)
     back0 = volume_back(x0, slopes1, elements)
-    start = 0.5 * w + w1 + step_size * back0
+    start = w1 - 0.5 * w + step_size * back0
 
     local1 = outer_local(t1)
     rate1 = volume(x1, d_high, d_low, elements)
     e1 = outer(t1, local1, net.wait(2))
-    rate1 = rate1 + lift_factor * lift(jump(t1, e1), select_t, elements)
-    net.output(0, from_rows(0.5 * x0 + 0.5 * (x1 + step_size * rate1), elements))
+    rate1 = rate1 + lift_factor * lift(jump(t1, e1), elements)
+    net.output(0, 0.5 * (x1 - x0) + 0.5 * step_size * rate1)
 
     in_bar = in_bar + dot(unpick, net.wait(3))
-    start = start + step_size * lift(in_bar, select_t, elements)
-    net.output(1, from_rows(start, elements))
+    start = start + step_size * lift(in_bar, elements)
+    net.output(1, start)
 
 
 class Net:
-    def __init__(self, n_dom, n_sub, outs, send_bufs, recv_bufs, send_sem, recv_sem):
+    def __init__(
+        self, n_dom, n_sub, inputs, held, send_bufs, recv_bufs, send_sem, recv_sem, load_sem
+    ):
         self.n_dom, self.n_sub = n_dom, n_sub
         self.dom, self.sub = lax.axis_index("dom"), lax.axis_index("sub")
-        self.outs = outs
         self.send_bufs, self.recv_bufs = send_bufs, recv_bufs
         self.send_sem, self.recv_sem = send_sem, recv_sem
         self.greeted = False
+        self.held = held
+        self.loads = [
+            pltpu.make_async_copy(inputs[n], held[n], load_sem.at[n]) for n in range(len(held))
+        ]
+        for load in self.loads:
+            load.start()
+
+    def load(self, which):
+        self.loads[which].wait()
+        return self.held[which][...]
 
     def partners(self):
         for group in (0, 2, 1):
@@ -407,21 +441,32 @@
         for phase in range(4):
             for copy in self.copies(phase):
                 copy.wait_send()
-
-    def output(self, which, parts):
-        for t in range(3):
-            for half in range(2):
-                if 2 * t + half < 5:
-                    self.outs[which][2 * t + half] = parts[t][64 * half : 64 * (half + 1)]
+        for store in self.stores:
+            store.wait()
+
+    def output(self, which, x):
+        elements = x.shape[0] // 3
+        for member in range(5):
+            tile, half = member // 2, member % 2
+            self.staged[5 * which + member] = x[
+                elements * tile : elements * (tile + 1), 64 * half : 64 * (half + 1)
+            ]
+        self.stores[which].start()
 
 
 def kernel(n_dom, n_sub, *refs):
-    state, final, slots, ext_row, ext, perm = refs[:6]
-    mats = refs[6:12]
-    outs = refs[12:14]
+    inputs, out, held, staged = refs[:6], refs[6], refs[7:13], refs[13]
     send_bufs, recv_bufs = refs[14:18], refs[18:22]
-    net = Net(n_dom, n_sub, outs, send_bufs, recv_bufs, refs[22], refs[23])
-    program(state[...], final[...], slots[...], ext_row[...], ext[...], perm[...], mats, net)
+    send_sem, recv_sem, load_sem, store_sem = refs[22:]
+    net = Net(n_dom, n_sub, inputs, held, send_bufs, recv_bufs, send_sem, recv_sem, load_sem)
+    net.staged = staged
+    net.stores = [
+        pltpu.make_async_copy(
+            staged.at[pl.ds(5 * n, 5)], out.at[pl.ds(5 * n, 5)], store_sem.at[n]
+        )
+        for n in range(2)
+    ]
+    program(net)
     net.finish()
 
 
@@ -431,33 +476,40 @@
 
     def shards(state, final, send_slot, ext_index, ext_perm):
         n_slots = send_slot.shape[1]
-        widths = (LANES, 4 * LANES, LANES, LANES)
-        vmem = pl.BlockSpec(memory_space=pltpu.VMEM)
+        widths = (LANES, 3 * LANES, LANES, LANES)
         buffers = [pltpu.VMEM((n_slots, width), BF16) for width in widths]
-        result = jax.ShapeDtypeStruct(state.shape, F32)
-        return pl.pallas_call(
+        operands = [
+            state.transpose(0, 2, 1),
+            send_slot,
+            ext_index,
+            ext_perm,
+            final.transpose(0, 2, 1),
+            jnp.asarray(mats),
+        ]
+        elements = state.shape[2]
+        result = jax.ShapeDtypeStruct((10, elements, 64), F32)
+        hbm = pl.BlockSpec(memory_space=pltpu.HBM)
+        change = pl.pallas_call(
             lambda *refs: kernel(n_dom, n_sub, *refs),
-            out_shape=(result, result),
-            in_specs=[vmem] * 12,
-            out_specs=(vmem, vmem),
-            scratch_shapes=buffers
+            out_shape=result,
+            in_specs=[hbm] * 6,
+            out_specs=hbm,
+            scratch_shapes=[pltpu.VMEM(x.shape, x.dtype) for x in operands]
+            + [pltpu.VMEM((10, elements, 64), F32)]
+            + buffers
             + buffers
             + [
                 pltpu.SemaphoreType.DMA((4, 3 * n_sub)),
                 pltpu.SemaphoreType.DMA((4, 3 * n_sub)),
+                pltpu.SemaphoreType.DMA((6,)),
+                pltpu.SemaphoreType.DMA((2,)),
             ],
             compiler_params=pltpu.CompilerParams(
-                collective_id=0, has_side_effects=True, vmem_limit_bytes=32 * 1024 * 1024
+                collective_id=0, has_side_effects=True, vmem_limit_bytes=60 * 1024 * 1024
             ),
-        )(
-            state,
-            final,
-            send_slot,
-            ext_index.reshape(1, -1),
-            ext_index,
-            ext_perm,
-            *[jnp.asarray(m) for m in mats],
-        )
+        )(*operands)
+        change = change.transpose(0, 2, 1)
+        return state + change[:5], final + change[5:]
 
     return jax.shard_map(
         shards,

time: 29.7 us -> 23.4 us (0.79)
  local copies, waits for them, and re-layouts: 7.77 us -> 0.01 us
  other arithmetic: 0 us -> 1.6 us
    unnamed x20 -> x4, local copies, waits for them, and re-layouts: 5.46 us -> 0.01 us
    add x0 -> x1, other arithmetic: none -> 1.6 us  [shards(): return (state + change[:5], final + change[5:])]
    pallas_call x2 -> x0, local copies, waits for them, and re-layouts: 1.49 us -> none  [shards(): pl.pallas_call(lambda *refs: kernel(n_dom, n_sub, *refs), out_shape=(resu...]
    reshape x1 -> x0, local copies, waits for them, and re-layouts: 0.82 us -> none  [shards(): ext_index.reshape(1, -1)]
where the time goes in v2:
time: 23.4 us; the launch traced here: 23.3 us
  Pallas kernels  21 us (90%)
  other arithmetic  1.6 us (7%)
  between operations  0.67 us (3%)
    pallas_call x1, Pallas kernels, shards(): pl.pallas_call(lambda *refs: kernel(n_dom, n_sub, *refs), out_shape=resul...  21 us
    add x1, other arithmetic, shards(): return (state + change[:5], final + change[5:])  1.6 us

profile of v2, /device:TPU:0, one launch (start us, length us, event | category | flops | bytes accessed | tf_op | source)
XLA Modules:
  0.0 23.3 jit_solution(5318992387876132519)
XLA Ops:
  0.6 0.0 copy-start
  0.6 0.0 copy-start.1
  0.7 21.0 %shard_map.77 = f32[10,32,64]{2,1,0:T(8,128)} custom-call(f32[5,32,64]{2,1,0:T(8,128)} %bitcast.5, s32[1,192]{1,0:T(1,128)} %refs_1_.1, s32[6,32]{1,0:T(8,128)} %refs_2_.1, s32[6,32]{1,0:T(8,128)} %refs_3_.1, f32[5,32,64]{2,1,0:T(8,128)} %bitcast.4, bf16[1536,128]{1,0:T(8,128)(2,1)} %constant.2.clone.refs_5_), custom_call_target="tpu_custom_call" | custom-call | tf_op jit(solution)/shard_map/pallas_call | solution.py:492
  21.7 0.0 copy-done
  21.7 0.0 copy-done.1
  21.7 1.6 %slice_add_fusion = (f32[5,64,32]{1,2,0:T(8,128)}, f32[5,64,32]{1,2,0:T(8,128)}) fusion(f32[5,64,32]{1,2,0:T(8,128)S(1)} %copy-done, f32[10,64,32]{1,2,0:T(8,128)} %bitcast.3, f32[5,64,32]{1,2,0:T(8,128)S(1)} %copy-done.1), kind=kLoop, calls=%fused_computation | loop fusion | flops 20480 | bytes 245760 | tf_op jit(solution)/shard_map/add | solution.py:512
Async XLA Ops:
  0.6 21.0 %copy-start = (f32[5,64,32]{1,2,0:T(8,128)S(1)}, f32[5,64,32]{1,2,0:T(8,128)}, u32[]{:S(2)}) copy-start(f32[5,64,32]{1,2,0:T(8,128)} %param.7) | copy-start | bytes 122884
  0.6 21.0 %copy-start.1 = (f32[5,64,32]{1,2,0:T(8,128)S(1)}, f32[5,64,32]{1,2,0:T(8,128)}, u32[]{:S(2)}) copy-start(f32[5,64,32]{1,2,0:T(8,128)} %param.6) | copy-start | bytes 122884

commit v3 on v2

--- a/solution.py
+++ b/solution.py
@@ -199,21 +199,24 @@
             q * (speed + self.drift) + self.ends * speed + jnp.where(self.normal, pressure, 0.0)
         )
 
-    def back(self, q, w, axis=None):
+    def place(self, axis):
         if axis is None:
-            at, drift, normal = self.at_speed, self.drift, self.normal
-        else:
-            at = (1 + axis) * 16 + self.node
-            drift = mean_flow if axis == 0 else 0.0
-            normal = self.member == 1 + axis
-        product = (q + self.ends) * w
+            return self.at_speed, self.drift, self.normal
+        drift = mean_flow if axis == 0 else 0.0
+        return (1 + axis) * 16 + self.node, drift, self.member == 1 + axis
+
+    def ready(self, q, axis=None):
+        at, drift, _ = self.place(axis)
+        return lanes_of(q, at) + drift, q + self.ends
+
+    def back(self, prepared, w, axis=None):
+        at, _, normal = self.place(axis)
+        speed, weights = prepared
+        product = weights * w
         for shift in (64, 32, 16):
             product = product + pltpu.roll(product, shift, 1)
-        term = (lanes_of(q, at) + drift) * w + jnp.where(normal, product, 0.0)
+        term = speed * w + jnp.where(normal, product, 0.0)
         return term + jnp.where(self.member == 4, lanes_of(w, at), 0.0)
-
-    def jump(self, inner, outer):
-        return 0.5 * (self.flux(inner) - self.flux(outer)) + (outer - inner)
 
 
 def column(values):
@@ -252,18 +255,12 @@
     swap = (perm_column & 4) != 0
     base = faces.member * 16
     r, s = faces.node // 4, faces.node % 4
-    r_new = jnp.where(flip_r, 3 - r, r)
-    s_new = jnp.where(flip_s, 3 - s, s)
-    orient = base + jnp.where(swap, 4 * s_new + r_new, 4 * r_new + s_new)
     r_old = jnp.where(swap, s, r)
     s_old = jnp.where(swap, r, s)
     r_old = jnp.where(flip_r, 3 - r_old, r_old)
     s_old = jnp.where(flip_s, 3 - s_old, s_old)
     unorient = base + 4 * r_old + s_old
-
-    to_local = one_hot(ext_row == iota((n_faces, n_faces), 0))
     to_slots = one_hot(ext_row - n_faces == iota((n_slots, n_faces), 0))
-    unpick = one_hot(slots == iota((n_faces, n_slots), 0))
 
     w = to_rows(net.load(4))
     w_jump = lift_factor * traces(w, elements)
@@ -290,6 +287,11 @@
     cot_high, cot_low = halves(by_axis(w_turned))
     net.send(1, lambda: dot(to_slots, cot_high).astype(BF16))
 
+    r_new = jnp.where(flip_r, 3 - r, r)
+    s_new = jnp.where(flip_s, 3 - s, s)
+    orient = base + jnp.where(swap, 4 * s_new + r_new, 4 * r_new + s_new)
+    to_local = one_hot(ext_row == iota((n_faces, n_faces), 0))
+    unpick = one_hot(slots == iota((n_faces, n_slots), 0))
     from_local = one_hot(ext_column == iota((n_faces, n_faces), 1))
     from_slots = one_hot(ext_column - n_faces == iota((n_faces, n_slots), 1))
 
@@ -301,8 +303,8 @@
         e = lanes_of(local + dot(from_slots, received), orient)
         return jnp.where(wall, t * faces.mirror, e)
 
-    def jump(t, e):
-        return faces.jump(t, e)
+    def half(t):
+        return 0.5 * faces.flux(t) - t
 
     local0 = outer_local(t0)
     size = 3 * LANES
@@ -316,27 +318,32 @@
     cot_local = dot(to_local, cot_high) + dot(to_local, cot_low) - by_axis(w_jump)
     slopes = dot_stacked(w, b_high, b_low)
 
+    base0 = x0 + step_size * rate0
+    half0 = half(t0)
+    ready0 = faces.ready(t0)
     e0 = outer(t0, local0, net.wait(0))
-    x1 = x0 + step_size * (rate0 + lift_factor * lift(jump(t0, e0), elements))
+    x1 = base0 + step_size * lift_factor * lift(half0 - half(e0), elements)
     t1 = traces(x1, elements)
     net.send(2, lambda: dot(pick, t1.astype(BF16)).astype(BF16))
 
     back1 = volume_back(x1, slopes, elements)
-    wall_out = w_jump - 0.5 * faces.sign * faces.back(t1 * faces.mirror, w_jump)
+    wall_out = w_jump - 0.5 * faces.sign * faces.back(faces.ready(t1 * faces.mirror), w_jump)
     t_bar = jnp.where(wall, faces.mirror * wall_out, 0.0)
+    ready1 = [faces.ready(t1, a) for a in range(3)]
+    ready_e0 = faces.ready(e0)
     cot_all = unpacked(cot_local + dot(unpick, net.wait(1)))
     t_bar = t_bar + cot_all[3]
     for a in range(3):
-        t_bar = t_bar - 0.5 * faces.back(t1, cot_all[a], a)
+        t_bar = t_bar - 0.5 * faces.back(ready1[a], cot_all[a], a)
     w1 = 0.5 * w + 0.5 * step_size * (back1 + lift(t_bar, elements))
 
     w1_jump = lift_factor * traces(w1, elements)
-    out_bar = w1_jump - 0.5 * faces.sign * faces.back(e0, w1_jump)
+    out_bar = w1_jump - 0.5 * faces.sign * faces.back(ready_e0, w1_jump)
     turned = lanes_of(jnp.where(wall, 0.0, out_bar), unorient)
     turned_high, turned_low = halves(turned)
     net.send(3, lambda: dot(to_slots, turned_high).astype(BF16))
 
-    in_bar = 0.5 * faces.sign * faces.back(t0, w1_jump) - w1_jump
+    in_bar = 0.5 * faces.sign * faces.back(ready0, w1_jump) - w1_jump
     in_bar = in_bar + jnp.where(wall, faces.mirror * out_bar, 0.0)
     in_bar = in_bar + dot(to_local, turned_high) + dot(to_local, turned_low)
     slopes1 = dot_stacked(w1, b_high, b_low)
@@ -345,8 +352,9 @@
 
     local1 = outer_local(t1)
     rate1 = volume(x1, d_high, d_low, elements)
+    half1 = half(t1)
     e1 = outer(t1, local1, net.wait(2))
-    rate1 = rate1 + lift_factor * lift(jump(t1, e1), elements)
+    rate1 = rate1 + lift_factor * lift(half1 - half(e1), elements)
     net.output(0, 0.5 * (x1 - x0) + 0.5 * step_size * rate1)
 
     in_bar = in_bar + dot(unpick, net.wait(3))
@@ -374,10 +382,11 @@
         self.loads[which].wait()
         return self.held[which][...]
 
-    def partners(self):
-        for group in (0, 2, 1):
+    def partners(self, way=1):
+        first = way * (2 * lax.rem(self.dom, 2) - 1)
+        for group, ahead in ((1 + first, True), (1 - first, True), (1, False)):
             for j in range(self.n_sub):
-                if group != 1 or j != 0:
+                if ahead or j != 0:
                     yield group, lax.rem(self.sub + j, self.n_sub)
 
     def neighbour(self, steps):
@@ -397,7 +406,7 @@
         source, target = self.send_bufs[phase], self.recv_bufs[phase]
         size = source.shape[0] // (3 * self.n_sub)
         way = 1 if phase % 2 == 0 else -1
-        for group, other in self.partners():
+        for group, other in self.partners(way):
             there = pl.multiple_of((group * self.n_sub + other) * size, size)
             here = pl.multiple_of((group * self.n_sub + self.sub) * size, size)
             yield pltpu.make_async_remote_copy(

time: 23.4 us -> 23.3 us (level)
  no operation moved by 1% of the time
where the time goes in v3:
time: 23.3 us; the launch traced here: 23.1 us
  Pallas kernels  20.9 us (90%)
  other arithmetic  1.6 us (7%)
  between operations  0.67 us (3%)
    pallas_call x1, Pallas kernels, shards(): pl.pallas_call(lambda *refs: kernel(n_dom, n_sub, *refs), out_shape=resul...  20.9 us
    add x1, other arithmetic, shards(): return (state + change[:5], final + change[5:])  1.6 us

profile of v3, /device:TPU:0, one launch (start us, length us, event | category | flops | bytes accessed | tf_op | source)
XLA Modules:
  0.0 23.1 jit_solution(3252468234672912783)
XLA Ops:
  0.6 0.0 copy-start
  0.6 0.0 copy-start.1
  0.7 20.9 %shard_map.77 = f32[10,32,64]{2,1,0:T(8,128)} custom-call(f32[5,32,64]{2,1,0:T(8,128)} %bitcast.5, s32[1,192]{1,0:T(1,128)} %refs_1_.1, s32[6,32]{1,0:T(8,128)} %refs_2_.1, s32[6,32]{1,0:T(8,128)} %refs_3_.1, f32[5,32,64]{2,1,0:T(8,128)} %bitcast.4, bf16[1536,128]{1,0:T(8,128)(2,1)} %constant.2.clone.refs_5_), custom_call_target="tpu_custom_call" | custom-call | tf_op jit(solution)/shard_map/pallas_call | solution.py:501
  21.5 0.0 copy-done
  21.5 0.0 copy-done.1
  21.5 1.6 %slice_add_fusion = (f32[5,64,32]{1,2,0:T(8,128)}, f32[5,64,32]{1,2,0:T(8,128)}) fusion(f32[5,64,32]{1,2,0:T(8,128)S(1)} %copy-done, f32[10,64,32]{1,2,0:T(8,128)} %bitcast.3, f32[5,64,32]{1,2,0:T(8,128)S(1)} %copy-done.1), kind=kLoop, calls=%fused_computation | loop fusion | flops 20480 | bytes 245760 | tf_op jit(solution)/shard_map/add | solution.py:521
Async XLA Ops:
  0.6 20.9 %copy-start = (f32[5,64,32]{1,2,0:T(8,128)S(1)}, f32[5,64,32]{1,2,0:T(8,128)}, u32[]{:S(2)}) copy-start(f32[5,64,32]{1,2,0:T(8,128)} %param.7) | copy-start | bytes 122884
  0.6 20.9 %copy-start.1 = (f32[5,64,32]{1,2,0:T(8,128)S(1)}, f32[5,64,32]{1,2,0:T(8,128)}, u32[]{:S(2)}) copy-start(f32[5,64,32]{1,2,0:T(8,128)} %param.6) | copy-start | bytes 122884

commit v4 on v3

--- a/solution.py
+++ b/solution.py
@@ -348,14 +348,15 @@
     in_bar = in_bar + dot(to_local, turned_high) + dot(to_local, turned_low)
     slopes1 = dot_stacked(w1, b_high, b_low)
     back0 = volume_back(x0, slopes1, elements)
-    start = w1 - 0.5 * w + step_size * back0
+    start = 0.5 * w + w1 + step_size * back0
 
     local1 = outer_local(t1)
     rate1 = volume(x1, d_high, d_low, elements)
     half1 = half(t1)
     e1 = outer(t1, local1, net.wait(2))
     rate1 = rate1 + lift_factor * lift(half1 - half(e1), elements)
-    net.output(0, 0.5 * (x1 - x0) + 0.5 * step_size * rate1)
+    net.output(0, 0.5 * x0 + 0.5 * (x1 + step_size * rate1))
+    net.sent((0, 1, 2))
 
     in_bar = in_bar + dot(unpick, net.wait(3))
     start = start + step_size * lift(in_bar, elements)
@@ -446,10 +447,13 @@
             ).wait_recv()
         return target[...]
 
-    def finish(self):
-        for phase in range(4):
+    def sent(self, phases):
+        for phase in phases:
             for copy in self.copies(phase):
                 copy.wait_send()
+
+    def finish(self):
+        self.sent((3,))
         for store in self.stores:
             store.wait()
 
@@ -477,6 +481,17 @@
     ]
     program(net)
     net.finish()
+
+
+def hand_out(both, first, second, sems):
+    copies = [
+        pltpu.make_async_copy(both.at[pl.ds(5 * n, 5)], out, sems.at[n])
+        for n, out in enumerate((first, second))
+    ]
+    for copy in copies:
+        copy.start()
+    for copy in copies:
+        copy.wait()
 
 
 def solution(mesh):
@@ -498,7 +513,7 @@
         elements = state.shape[2]
         result = jax.ShapeDtypeStruct((10, elements, 64), F32)
         hbm = pl.BlockSpec(memory_space=pltpu.HBM)
-        change = pl.pallas_call(
+        both = pl.pallas_call(
             lambda *refs: kernel(n_dom, n_sub, *refs),
             out_shape=result,
             in_specs=[hbm] * 6,
@@ -517,8 +532,16 @@
                 collective_id=0, has_side_effects=True, vmem_limit_bytes=60 * 1024 * 1024
             ),
         )(*operands)
-        change = change.transpose(0, 2, 1)
-        return state + change[:5], final + change[5:]
+        single = jax.ShapeDtypeStruct((5, elements, 64), F32)
+        outs = pl.pallas_call(
+            hand_out,
+            out_shape=(single, single),
+            in_specs=[hbm],
+            out_specs=(hbm, hbm),
+            scratch_shapes=[pltpu.SemaphoreType.DMA((2,))],
+            compiler_params=pltpu.CompilerParams(vmem_limit_bytes=60 * 1024 * 1024),
+        )(both)
+        return tuple(x.transpose(0, 2, 1) for x in outs)
 
     return jax.shard_map(
         shards,

time: 23.3 us -> 27.7 us (1.19)
  Pallas kernels: 20.9 us -> 26.9 us
  other arithmetic: 1.6 us -> 0 us
    pallas_call x0 -> x1, Pallas kernels: none -> 6.08 us  [shards(): pl.pallas_call(hand_out, out_shape=(single, single), in_specs=[hbm], out_...]
    add x1 -> x0, other arithmetic: 1.6 us -> none  [shards(): return (state + change[:5], final + change[5:])]
where the time goes in v4:
time: 27.7 us; the launch traced here: 27.6 us
  Pallas kernels  26.9 us (97%)
  between operations  0.64 us (2%)
    pallas_call x1, Pallas kernels, shards(): pl.pallas_call(lambda *refs: kernel(n_dom, n_sub, *refs), out_shape=resul...  20.9 us
    pallas_call x1, Pallas kernels, shards(): pl.pallas_call(hand_out, out_shape=(single, single), in_specs=[hbm], out_...  6.08 us

profile of v4, /device:TPU:0, one launch (start us, length us, event | category | flops | bytes accessed | tf_op | source)
XLA Modules:
  0.0 27.6 jit_solution(1197698115654445099)
XLA Ops:
  0.6 20.9 %shard_map.77.both = f32[10,32,64]{2,1,0:T(8,128)} custom-call(f32[5,32,64]{2,1,0:T(8,128)} %bitcast.4, s32[1,192]{1,0:T(1,128)} %refs_1_.1, s32[6,32]{1,0:T(8,128)} %refs_2_.1, s32[6,32]{1,0:T(8,128)} %refs_3_.1, f32[5,32,64]{2,1,0:T(8,128)} %bitcast.5, bf16[1536,128]{1,0:T(8,128)(2,1)} %constant.2.clone.refs_5_), custom_call_target="tpu_custom_call" | custom-call | tf_op jit(solution)/shard_map/pallas_call | solution.py:516
  21.5 6.1 %shard_map.78 = (f32[5,32,64]{2,1,0:T(8,128)}, f32[5,32,64]{2,1,0:T(8,128)}) custom-call(f32[10,32,64]{2,1,0:T(8,128)} %shard_map.77.both), custom_call_target="tpu_custom_call" | custom-call | tf_op jit(solution)/shard_map/pallas_call | solution.py:536

commit v5 on v4

--- a/solution.py
+++ b/solution.py
@@ -483,15 +483,23 @@
     net.finish()
 
 
-def hand_out(both, first, second, sems):
-    copies = [
-        pltpu.make_async_copy(both.at[pl.ds(5 * n, 5)], out, sems.at[n])
+def hand_out(both, first, second, held, load_sems, store_sems):
+    parts = [held.at[pl.ds(5 * n, 5)] for n in range(2)]
+    loads = [
+        pltpu.make_async_copy(both.at[pl.ds(5 * n, 5)], parts[n], load_sems.at[n])
+        for n in range(2)
+    ]
+    stores = [
+        pltpu.make_async_copy(parts[n], out, store_sems.at[n])
         for n, out in enumerate((first, second))
     ]
-    for copy in copies:
-        copy.start()
-    for copy in copies:
-        copy.wait()
+    for load in loads:
+        load.start()
+    for load, store in zip(loads, stores):
+        load.wait()
+        store.start()
+    for store in stores:
+        store.wait()
 
 
 def solution(mesh):
@@ -538,7 +546,11 @@
             out_shape=(single, single),
             in_specs=[hbm],
             out_specs=(hbm, hbm),
-            scratch_shapes=[pltpu.SemaphoreType.DMA((2,))],
+            scratch_shapes=[
+                pltpu.VMEM((10, elements, 64), F32),
+                pltpu.SemaphoreType.DMA((2,)),
+                pltpu.SemaphoreType.DMA((2,)),
+            ],
             compiler_params=pltpu.CompilerParams(vmem_limit_bytes=60 * 1024 * 1024),
         )(both)
         return tuple(x.transpose(0, 2, 1) for x in outs)

time: 27.7 us -> 23.3 us (0.84)
  Pallas kernels: 26.9 us -> 22.5 us
    pallas_call x1, Pallas kernels: 6.08 us -> 1.6 us  [shards(): pl.pallas_call(hand_out, out_shape=(single, single), in_specs=[hbm], out_...]
where the time goes in v5:
time: 23.3 us; the launch traced here: 23.1 us
  Pallas kernels  22.5 us (97%)
  between operations  0.64 us (3%)
    pallas_call x1, Pallas kernels, shards(): pl.pallas_call(lambda *refs: kernel(n_dom, n_sub, *refs), out_shape=resul...  20.9 us
    pallas_call x1, Pallas kernels, shards(): pl.pallas_call(hand_out, out_shape=(single, single), in_specs=[hbm], out_...  1.6 us

profile of v5, /device:TPU:0, one launch (start us, length us, event | category | flops | bytes accessed | tf_op | source)
XLA Modules:
  0.0 23.1 jit_solution(10794770723601387141)
XLA Ops:
  0.6 20.9 %shard_map.77.both = f32[10,32,64]{2,1,0:T(8,128)} custom-call(f32[5,32,64]{2,1,0:T(8,128)} %bitcast.4, s32[1,192]{1,0:T(1,128)} %refs_1_.1, s32[6,32]{1,0:T(8,128)} %refs_2_.1, s32[6,32]{1,0:T(8,128)} %refs_3_.1, f32[5,32,64]{2,1,0:T(8,128)} %bitcast.5, bf16[1536,128]{1,0:T(8,128)(2,1)} %constant.2.clone.refs_5_), custom_call_target="tpu_custom_call" | custom-call | tf_op jit(solution)/shard_map/pallas_call | solution.py:524
  21.5 1.6 %shard_map.78 = (f32[5,32,64]{2,1,0:T(8,128)}, f32[5,32,64]{2,1,0:T(8,128)}) custom-call(f32[10,32,64]{2,1,0:T(8,128)} %shard_map.77.both), custom_call_target="tpu_custom_call" | custom-call | tf_op jit(solution)/shard_map/pallas_call | solution.py:544
